TPU v7x, 256 devices: a whole 4x4x8 slice. The times are simulated.
256 devices in a mesh: lat: 4 (over y_hi, core), lon: 32 (over x, z), lev: 2 (over y_lo).
Axes of the slice: x: 4, y: 4 (y_hi: 2, y_lo: 2; y = y_hi * 2 + y_lo), z: 8, core: 2. Of those that a mesh axis runs over, the one named last changes fastest.
Arguments:
- levels_in: bfloat16 [4, 24, 768, 512], P('lev', 'lat', 'lon'), may hold values from -150 to 150, as said below
- enc_gain: bfloat16 [512], replicated, may hold values from 0.099609375 to 1.8984375
- latent_query: bfloat16 [2, 512], replicated, may hold values from -6 to 6
- w_query: bfloat16 [512, 512], replicated, may hold values from -16 to 16
- w_kv: bfloat16 [512, 1024], replicated, may hold values from -0.25 to 0.25
- w_cross_out: bfloat16 [512, 512], replicated, may hold values from -0.25 to 0.25
- shift_lat: int32 [1], replicated, may hold values from 0 to 5
- shift_lon: int32 [1], replicated, may hold values from 0 to 11
- attn_gain: bfloat16 [512], replicated, may hold values from 0.099609375 to 1.8984375
- w_qkv: bfloat16 [512, 1536], replicated, may hold values from -16 to 16
- w_proj: bfloat16 [512, 512], replicated, may hold values from -0.25 to 0.25
- mlp_gain: bfloat16 [512], replicated, may hold values from 0.099609375 to 1.8984375
- w_up: bfloat16 [512, 2048], replicated, may hold values from -0.25 to 0.25
- w_down: bfloat16 [2048, 512], replicated, may hold values from -0.125 to 0.125
- merge_gain: bfloat16 [2048], replicated, may hold values from 0.099609375 to 1.8984375
- w_merge: bfloat16 [2048, 1024], replicated, may hold values from -0.125 to 0.125
Outputs:
- merged: bfloat16 [2, 12, 384, 1024], P(None, 'lat', ('lon', 'lev'))
Inputs may be any that keep to these rules, and one draw needn't show every extreme that they name: `levels_in`: level tokens of varying magnitude from token to token and from feature to feature.
All inputs are finite; a program needn't handle non-finite values.
Results may differ from a plain program's by a relative error of at most 0.015.
The roundings to bfloat16 on the way count: a program that leaves them out, or rounds other values in their place, can miss the bound.
Values may be sent and summed in bfloat16 or wider, within the bound.
No kernel may reach another device: no remote copies, remote signals or barrier semaphores. Data moves between devices by JAX's collectives and lax.ppermute only.
A program may use at most 128 MiB of HBM per device.

v0:
```python
import math

import jax
import jax.numpy as jnp
from jax import lax
from jax.sharding import PartitionSpec as P

HEADS = 16
WH = 6
WW = 12


EPSILON = 1e-05
NEG_LARGE = -1e30


def extended(block, sides, width, periodic):
    for axis, dim in sides:
        count = lax.axis_size(axis)
        forward = [(i, i + 1) for i in range(count - 1)]
        if periodic:
            forward.append((count - 1, 0))
        backward = [(target, source) for source, target in forward]
        low = lax.ppermute(
            lax.slice_in_dim(block, block.shape[dim] - width, None, axis=dim), axis, forward
        )
        high = lax.ppermute(lax.slice_in_dim(block, 0, width, axis=dim), axis, backward)
        block = jnp.concatenate([low, block, high], axis=dim)
    return block


def layer_norm(values, gain_vec):
    values = values.astype(jnp.float32)
    centre = values - jnp.mean(values, axis=-1, keepdims=True)
    spread = jnp.mean(centre * centre, axis=-1, keepdims=True)
    return centre * lax.rsqrt(spread + EPSILON) * gain_vec.astype(jnp.float32)


def project(values, weight):
    lead_shape = values.shape[:-1]
    flat_rows = values.reshape(-1, values.shape[-1])
    product = jnp.dot(flat_rows, weight, preferred_element_type=jnp.float32)
    return product.reshape(lead_shape + (weight.shape[1],))


def encode(tokens, enc_gain, queries, latent_query, w_kv, w_cross_out):
    level_count, row_total, col_total, feat_width = tokens.shape
    head_dim = feat_width // HEADS
    normed = layer_norm(tokens, enc_gain).astype(jnp.bfloat16)
    keyval = project(normed, w_kv).astype(jnp.bfloat16)
    key_part = keyval[..., :feat_width].reshape(level_count, row_total, col_total, HEADS, head_dim)
    value_part = keyval[..., feat_width:].reshape(
        level_count, row_total, col_total, HEADS, head_dim
    )
    query_heads = queries.reshape(-1, HEADS, head_dim)
    scores = jnp.einsum(
        "khe,lrche->rchkl", query_heads, key_part, preferred_element_type=jnp.float32
    ) / math.sqrt(head_dim)
    weights = jax.nn.softmax(scores, axis=-1).astype(jnp.bfloat16)
    attended = jnp.einsum(
        "rchkl,lrche->krche", weights, value_part, preferred_element_type=jnp.float32
    )
    attended = attended.astype(jnp.bfloat16).reshape(-1, row_total, col_total, feat_width)
    latents = latent_query.astype(jnp.float32)[:, None, None, :] + project(attended, w_cross_out)
    return latents.astype(jnp.bfloat16)


def merge_patches(block_out, merge_gain, w_merge):
    latent_count, row_total, col_total, feat_width = block_out.shape
    grouped = block_out.reshape(latent_count, row_total // 2, 2, col_total // 2, 2, feat_width)
    grouped = grouped.transpose(0, 1, 3, 4, 2, 5).reshape(
        latent_count, row_total // 2, col_total // 2, 4 * feat_width
    )
    merge_in = layer_norm(grouped, merge_gain).astype(jnp.bfloat16)
    return project(merge_in, w_merge).astype(jnp.bfloat16)


def on_device(
    levels_in,
    enc_gain,
    latent_query,
    w_query,
    w_kv,
    w_cross_out,
    shift_lat,
    shift_lon,
    attn_gain,
    w_qkv,
    w_proj,
    mlp_gain,
    w_up,
    w_down,
    merge_gain,
    w_merge,
):
    queries = jnp.dot(latent_query, w_query, preferred_element_type=jnp.float32).astype(
        jnp.bfloat16
    )
    regrouped = lax.all_to_all(levels_in, "lev", split_axis=2, concat_axis=0, tiled=True)
    latents = encode(regrouped, enc_gain, queries, latent_query, w_kv, w_cross_out)
    latent_count, local_rows, local_cols, feat_width = latents.shape
    total_rows = local_rows * lax.axis_size("lat")
    row_anchor = lax.axis_index("lat") * local_rows
    col_anchor = lax.axis_index(("lon", "lev")) * local_cols
    shift_row = shift_lat[0]
    shift_col = shift_lon[0]
    row_offset = (row_anchor + shift_row) % WH
    col_offset = (col_anchor + shift_col) % WW
    row_start = WH - row_offset
    col_start = WW - col_offset
    span_rows = local_rows + WH
    span_cols = local_cols + WW
    padded = extended(latents, (("lat", 1),), WH, False)
    padded = extended(padded, ((("lon", "lev"), 2),), WW, True)
    row_part = lax.dynamic_slice_in_dim(padded, row_start, span_rows, 1)
    normed = layer_norm(
        lax.dynamic_slice_in_dim(row_part, col_start, span_cols, 2), attn_gain
    ).astype(jnp.bfloat16)
    qkv = project(normed, w_qkv).astype(jnp.bfloat16)
    global_rows = row_anchor - row_offset + jnp.arange(span_rows, dtype=jnp.int32)
    inside = (global_rows >= 0) & (global_rows < total_rows)
    qkv = jnp.where(inside[None, :, None, None], qkv, jnp.zeros_like(qkv))
    row_label = jnp.where(inside, 0, -1).astype(jnp.int32)
    row_windows = span_rows // WH
    col_windows = span_cols // WW
    window_count = row_windows * col_windows
    token_count = latent_count * WH * WW
    head_dim = feat_width // HEADS
    blocked = qkv.reshape(latent_count, row_windows, WH, col_windows, WW, 3 * feat_width)
    blocked = blocked.transpose(1, 3, 0, 2, 4, 5).reshape(window_count, token_count, 3 * feat_width)
    labels = row_label.reshape(row_windows, WH)
    labels = jnp.broadcast_to(
        labels[:, None, None, :, None], (row_windows, col_windows, latent_count, WH, WW)
    )
    labels = labels.reshape(window_count, token_count)
    allowed = labels[:, :, None] == labels[:, None, :]
    query_part = blocked[..., :feat_width].reshape(window_count, token_count, HEADS, head_dim)
    key_part = blocked[..., feat_width : 2 * feat_width].reshape(
        window_count, token_count, HEADS, head_dim
    )
    value_part = blocked[..., 2 * feat_width :].reshape(window_count, token_count, HEADS, head_dim)
    scores = jnp.einsum(
        "wqhe,wkhe->whqk", query_part, key_part, preferred_element_type=jnp.float32
    ) / math.sqrt(head_dim)
    scores = jnp.where(allowed[:, None], scores, NEG_LARGE)
    weights = jax.nn.softmax(scores, axis=-1).astype(jnp.bfloat16)
    window_out = jnp.einsum(
        "whqk,wkhe->wqhe", weights, value_part, preferred_element_type=jnp.float32
    )
    window_out = window_out.astype(jnp.bfloat16).reshape(
        row_windows, col_windows, latent_count, WH, WW, feat_width
    )
    window_out = window_out.transpose(2, 0, 3, 1, 4, 5).reshape(
        latent_count, span_rows, span_cols, feat_width
    )
    window_out = lax.dynamic_slice_in_dim(window_out, row_offset, local_rows, 1)
    window_out = lax.dynamic_slice_in_dim(window_out, col_offset, local_cols, 2)
    middle = latents.astype(jnp.float32) + project(window_out, w_proj)
    mlp_in = layer_norm(middle, mlp_gain).astype(jnp.bfloat16)
    hidden = jax.nn.gelu(project(mlp_in, w_up)).astype(jnp.bfloat16)
    block_out = (middle + project(hidden, w_down)).astype(jnp.bfloat16)
    return merge_patches(block_out, merge_gain, w_merge)


def solution(mesh):
    in_specs = (
        P("lev", "lat", "lon", None),
        P(),
        P(),
        P(),
        P(),
        P(),
        P(),
        P(),
        P(),
        P(),
        P(),
        P(),
        P(),
        P(),
        P(),
        P(),
    )
    out_specs = P(None, "lat", ("lon", "lev"), None)
    return jax.shard_map(
        on_device, mesh=mesh, in_specs=in_specs, out_specs=out_specs, check_vma=False
    )
```

profile of v0, /device:TPU:1, one launch (start us, length us, event | category | flops | bytes accessed | tf_op | source)
XLA Modules:
  0.0 123.5 jit_solution(13898172567928273081)
XLA Ops:
  0.0 1.9 %copy.110 = bf16[2,6,24,512]{3,1,0,2:T(8,128)(2,1)} copy(bf16[2,6,24,512]{3,2,1,0:T(8,128)(2,1)} %param.16) | data formatting | bytes 589824 | tf_op args[0]
  2.0 3.5 %all-to-all-start = ((bf16[2,6,24,512]{3,1,0,2:T(8,128)(2,1)}), bf16[2,6,24,512]{3,1,0,2:T(8,128)(2,1)S(1)}, u32[]{:S(2)}, u32[]{:S(2)}) async-start(bf16[2,6,24,512]{3,1,0,2:T(8,128)(2,1)} %copy.110), calls=%async_computation | async-start | bytes 786432 | tf_op jit(solution)/shard_map/all_to_all | solution.py:99
  5.4 0.7 convert_element_type.122
  6.1 0.7 convert_element_type.116
  6.8 1.2 convolution_convert_fusion.3
  8.1 2.7 %all-to-all-done = bf16[2,6,24,512]{3,1,0,2:T(8,128)(2,1)S(1)} async-done(((bf16[2,6,24,512]{3,1,0,2:T(8,128)(2,1)}), bf16[2,6,24,512]{3,1,0,2:T(8,128)(2,1)S(1)}, u32[]{:S(2)}, u32[]{:S(2)}) %all-to-all-start) | async-done | bytes 294944 | tf_op jit(solution)/shard_map/all_to_all | solution.py:99
  10.8 0.2 copy_convert_fusion
  11.0 0.5 copy.112
  11.4 0.2 reduce_sum.90
  11.7 0.5 multiply_reduce_fusion
  12.2 0.2 copy.115
  12.3 0.2 copy.113
  12.6 0.2 copy.119
  12.7 0.1 copy.120
  12.9 0.1 copy.116
  13.0 0.5 reshape.217
  13.5 0.2 multiply_convert_fusion
  13.8 1.8 %convolution_convert_fusion.1 = bf16[4,6,12,1024]{3,2,1,0:T(8,128)(2,1)S(1)} fusion(bf16[512,1024]{1,0:T(8,128)(2,1)} %param.20, bf16[4,6,12,512]{3,0,2,1:T(4,128)(2,1)S(1)} %multiply_convert_fusion), kind=kOutput, calls=%fused_computation.40 | convolution fusion | flops 302284800 | bytes 1933312 | tf_op jit(solution)/shard_map/dot_general | solution.py:42
  15.7 1.7 %reshape.232 = bf16[4,6,12,16,32]{4,3,2,1,0:T(8,128)(2,1)} reshape(bf16[4,6,12,512]{3,2,1,0:T(8,128)(2,1)S(1)} %get-tuple-element.11) | data formatting | bytes 589824 | tf_op jit(solution)/shard_map/reshape | solution.py:51
  17.4 5.1 %fusion.95 = (f32[6,12,16,2]{1,3,0,2:T(2,128)S(1)}, f32[6,12,16,2,4]{1,3,0,4,2:T(2,128)S(1)}) fusion(bf16[2,16,32,1,1]{2,1,0,4,3:T(8,128)(2,1)S(1)} %bitcast.113, bf16[4,6,12,16,32]{4,3,2,1,0:T(8,128)(2,1)} %reshape.232), kind=kOutput, calls=%fused_computation.110 | convolution fusion | flops 605952 | bytes 343040 | tf_op jit(solution)/shard_map/khe,lrche->rchkl/dot_general | solution.py:56
  22.5 0.3 fusion.76
  22.8 0.3 divide_convert_fusion.6
  23.1 1.7 %copy.127 = bf16[6,12,16,2,4]{4,3,2,1,0:T(2,128)(2,1)S(1)} copy(bf16[6,12,16,2,4]{1,3,0,4,2:T(2,128)(2,1)S(1)} %divide_convert_fusion.6) | data formatting | bytes 36864 | tf_op jit(solution)/shard_map/convert_element_type | solution.py:59
  24.8 1.7 %reshape.231 = bf16[4,6,12,16,32]{4,3,2,1,0:T(8,128)(2,1)} reshape(bf16[4,6,12,512]{3,2,1,0:T(8,128)(2,1)S(1)} %get-tuple-element.10) | data formatting | bytes 589824 | tf_op jit(solution)/shard_map/reshape | solution.py:52
  26.5 2.6 %fusion.34 = bf16[2,6,12,16,32]{4,0,3,2,1:T(2,128)(2,1)S(1)} fusion(bf16[6,12,16,2,4]{4,3,2,1,0:T(2,128)(2,1)S(1)} %copy.127, bf16[4,6,12,16,32]{4,3,2,1,0:T(8,128)(2,1)} %reshape.231), kind=kOutput, calls=%fused_computation.43 | convolution fusion | flops 663552 | bytes 460800 | tf_op jit(solution)/shard_map/rchkl,lrche->krche/dot_general | solution.py:60
  29.3 0.5 reshape.233
  29.9 0.4 copy-done.2
  30.2 0.3 fusion.54
  30.5 7.7 %collective-permute-start = (bf16[2,6,12,512]{3,2,1,0:T(8,128)(2,1)S(1)}, bf16[2,6,12,512]{3,2,1,0:T(8,128)(2,1)S(1)}, u32[]{:S(2)}, u32[]{:S(2)}) collective-permute-start(bf16[2,6,12,512]{3,2,1,0:T(8,128)(2,1)S(1)} %fusion.54), channel_id=1, source_target_pairs={{0,64},{64,128},{128,192},{1,65},{65,129},{129,193},{2,66},{66,130... | collective-permute-start | bytes 442376 | tf_op jit(solution)/shard_map/ppermute | solution.py:24
  38.2 1.9 %collective-permute-start.1 = (bf16[2,6,12,512]{3,2,1,0:T(8,128)(2,1)S(1)}, bf16[2,6,12,512]{3,2,1,0:T(8,128)(2,1)S(1)}, u32[]{:S(2)}, u32[]{:S(2)}) collective-permute-start(bf16[2,6,12,512]{3,2,1,0:T(8,128)(2,1)S(1)} %fusion.54), channel_id=1, source_target_pairs={{64,0},{128,64},{192,128},{65,1},{129,65},{193,129},{66,2},{130,66... | collective-permute-start | bytes 442376 | tf_op jit(solution)/shard_map/ppermute | solution.py:27
  41.5 12.4 %collective-permute-done.1 = bf16[2,6,12,512]{3,2,1,0:T(8,128)(2,1)S(1)} collective-permute-done((bf16[2,6,12,512]{3,2,1,0:T(8,128)(2,1)S(1)}, bf16[2,6,12,512]{3,2,1,0:T(8,128)(2,1)S(1)}, u32[]{:S(2)}, u32[]{:S(2)}) %collective-permute-start.1) | collective-permute-done | bytes 147488 | tf_op jit(solution)/shard_map/ppermute | solution.py:27
  54.0 0.5 copy.130
  54.5 0.3 collective-permute-start.2
  54.7 6.7 %collective-permute-start.3 = (bf16[2,18,12,512]{3,0,2,1:T(2,128)(2,1)S(1)}, bf16[2,18,12,512]{3,0,2,1:T(2,128)(2,1)}, u32[]{:S(2)}, u32[]{:S(2)}) collective-permute-start(bf16[2,18,12,512]{3,0,2,1:T(2,128)(2,1)S(1)} %copy.130), channel_id=1, source_target_pairs={{1,0},{2,1},{3,2},{4,3},{5,4},{6,5},{7,6},{8,7},{9,8},{10,9},{11,1... | collective-permute-start | bytes 1327112 | tf_op jit(solution)/shard_map/ppermute | solution.py:27
  61.7 0.8 broadcast_compare_fusion
  62.5 4.8 %collective-permute-done.2 = bf16[2,18,12,512]{3,0,2,1:T(2,128)(2,1)} collective-permute-done((bf16[2,18,12,512]{3,0,2,1:T(2,128)(2,1)S(1)}, bf16[2,18,12,512]{3,0,2,1:T(2,128)(2,1)}, u32[]{:S(2)}, u32[]{:S(2)}) %collective-permute-start.2) | collective-permute-done | bytes 442400 | tf_op jit(solution)/shard_map/ppermute | solution.py:24
  67.2 1.1 copy.132
  68.3 1.1 copy.133
  69.5 1.5 %convert_reduce_fusion = (f32[2,12,24]{2,1,0:T(8,128)S(1)}, bf16[2,12,24,512]{3,2,1,0:T(8,128)(2,1)S(1)}) fusion(s32[]{:T(128)S(6)} %select_n.49, s32[]{:T(128)S(6)} %select_n.52, bf16[2,18,12,512]{3,2,1,0:T(8,128)(2,1)S(1)} %copy.133, bf16[2,6,12,512]{3,2,1,0:T(8,128)(2,1)S(1)} %collective-permute-done.1, bf16[2,6,12,512]{3,2,1,0:T(8,128)(2,1)S(1)} %fusion.54, ...), kind=kLoop, calls=%fused_computation.37 | loop fusion | flops 3538368 | bytes 1919240 | tf_op jit(solution)/shard_map/reduce_sum | solution.py:34
  70.9 0.3 fusion.44
  71.3 1.2 fusion.8
  72.5 1.8 %copy.134 = bf16[2,12,24,1536]{3,0,2,1:T(2,128)(2,1)S(1)} copy(bf16[2,12,24,1536]{3,2,1,0:T(8,128)(2,1)S(1)} %fusion.8) | data formatting | bytes 3538944 | tf_op jit(solution)/shard_map/jit(_where)/select_n | solution.py:122
  74.3 2.7 %copy.135 = bf16[2,2,2,6,12,1536]{5,1,0,4,3,2:T(2,128)(2,1)} copy(bf16[2,2,2,6,12,1536]{5,2,4,1,3,0:T(2,128)(2,1)S(1)} %bitcast.102) | data formatting | bytes 3538944 | tf_op jit(solution)/shard_map/transpose | solution.py:130
  77.0 5.2 %reshape.211 = bf16[4,144,1536]{2,0,1:T(4,128)(2,1)} reshape(bf16[2,2,2,6,12,1536]{5,1,0,4,3,2:T(2,128)(2,1)} %copy.135) | data formatting | bytes 3538944 | tf_op jit(solution)/shard_map/reshape | solution.py:130
  82.2 2.9 %fusion.93 = (bf16[4,144,512]{2,0,1:T(4,128)(2,1)S(1)}, bf16[4,144,512]{2,0,1:T(4,128)(2,1)}, bf16[4,144,512]{2,0,1:T(4,128)(2,1)S(1)}) fusion(bf16[4,144,1536]{2,0,1:T(4,128)(2,1)} %reshape.211), kind=kLoop, calls=%fused_computation.108 | loop fusion | bytes 3538944 | tf_op jit(solution)/shard_map/slice | solution.py:138
  85.1 2.2 %copy.137 = bf16[4,144,512]{1,2,0:T(8,128)(2,1)} copy(bf16[4,144,512]{2,0,1:T(4,128)(2,1)} %get-tuple-element.8) | data formatting | bytes 1179648 | tf_op jit(solution)/shard_map/slice | solution.py:137
  87.3 1.4 %copy.138 = bf16[4,144,512]{1,2,0:T(8,128)(2,1)} copy(bf16[4,144,512]{2,0,1:T(4,128)(2,1)S(1)} %get-tuple-element.7) | data formatting | bytes 1179648 | tf_op jit(solution)/shard_map/slice | solution.py:138
  88.7 1.4 %copy.136 = bf16[4,144,512]{1,2,0:T(8,128)(2,1)} copy(bf16[4,144,512]{2,0,1:T(4,128)(2,1)S(1)} %get-tuple-element.9) | data formatting | bytes 1179648 | tf_op jit(solution)/shard_map/slice | solution.py:141
  90.1 9.5 %fusion.96 = (f32[4,16,144]{2,1,0:T(8,128)}, f32[4,16,144,144]{2,3,1,0:T(8,128)}) fusion(pred[4,144,144]{1,2,0:T(8,128)(4,1)S(1)} %copy-done.4, bf16[4,144,16,32]{1,3,2,0:T(8,128)(2,1)} %bitcast.107, bf16[4,144,16,32]{1,3,2,0:T(8,128)(2,1)} %bitcast.108), kind=kOutput, calls=%fused_computation.111 | convolution fusion | flops 90243216 | bytes 6607872 | tf_op jit(solution)/shard_map/sub | solution.py:146
  99.6 5.4 %fusion.33 = bf16[4,144,16,32]{1,3,2,0:T(8,128)(2,1)} fusion(bf16[4,144,16,32]{1,3,2,0:T(8,128)(2,1)S(1)} %bitcast.109, f32[4,16,144,144]{2,3,1,0:T(8,128)} %get-tuple-element.15, f32[4,16,144]{2,1,0:T(8,128)} %get-tuple-element.14), kind=kOutput, calls=%fused_computation.41 | convolution fusion | flops 87883776 | bytes 6524928 | tf_op jit(solution)/shard_map/whqk,wkhe->wqhe/dot_general | solution.py:147
  105.0 4.6 %copy.140 = bf16[4,144,16,32]{3,2,0,1:T(8,128)(2,1)} copy(bf16[4,144,16,32]{1,3,2,0:T(8,128)(2,1)} %fusion.33) | data formatting | bytes 1179648 | tf_op jit(solution)/shard_map/convert_element_type | solution.py:150
  109.6 4.2 %reshape.215 = bf16[2,2,2,6,12,512]{5,1,0,4,3,2:T(2,128)(2,1)S(1)} reshape(bf16[4,144,16,32]{3,2,0,1:T(8,128)(2,1)} %copy.140) | data formatting | bytes 1179648 | tf_op jit(solution)/shard_map/reshape | solution.py:150
  113.9 0.6 copy.141
  114.6 0.3 fusion.97
  115.0 0.2 multiply_reduce_fusion.1
  115.2 2.9 %fusion.51 = f32[2,6,12,512]{3,2,1,0:T(8,128)S(1)} fusion(f32[2,6,12,512]{3,2,1,0:T(8,128)S(1)} %get-tuple-element.17, bf16[2048,512]{1,0:T(8,128)(2,1)S(1)} %copy-done, bf16[512,2048]{1,0:T(8,128)(2,1)} %param.28, f32[512]{0:T(512)S(1)} %convert_element_type.138, f32[2,6,12]{2,1,0:T(8,128)S(1)} %add_rsqrt_fusion.3, ...), kind=kOutput, calls=%fused_computation.54 | convolution fusion | flops 607150080 | bytes 4787328 | tf_op jit(solution)/shard_map/dot_general | solution.py:42
  118.1 0.2 copy.143
  118.4 0.2 reduce_sum.98
  118.5 0.2 copy.144
  118.8 0.3 multiply_reduce_fusion.2
  119.1 0.4 reshape.218
  119.4 0.3 multiply_convert_fusion.4
  119.7 3.1 %fusion.55 = bf16[2,3,6,1024]{3,2,1,0:T(8,128)(2,1)S(1)} fusion(bf16[2048,1024]{1,0:T(8,128)(2,1)} %param.31, bf16[2,3,6,2048]{3,0,2,1:T(2,128)(2,1)S(1)} %multiply_convert_fusion.4), kind=kOutput, calls=%fused_computation.56 | convolution fusion | flops 151031808 | bytes 4415488 | tf_op jit(solution)/shard_map/dot_general | solution.py:42
  122.8 0.7 copy.146
  (39 shorter events, 0.8 us)
Async XLA Ops:
  0.0 115.2 %copy-start = (bf16[2048,512]{1,0:T(8,128)(2,1)S(1)}, bf16[2048,512]{1,0:T(8,128)(2,1)}, u32[]{:S(2)}) copy-start(bf16[2048,512]{1,0:T(8,128)(2,1)} %param.29) | copy-start | bytes 6291460
  2.0 8.9 %all-to-all-start = ((bf16[2,6,24,512]{3,1,0,2:T(8,128)(2,1)}), bf16[2,6,24,512]{3,1,0,2:T(8,128)(2,1)S(1)}, u32[]{:S(2)}, u32[]{:S(2)}) async-start(bf16[2,6,24,512]{3,1,0,2:T(8,128)(2,1)} %copy.110), calls=%async_computation | async-start | bytes 786432 | tf_op jit(solution)/shard_map/all_to_all | solution.py:99
  29.2 1.0 copy-start.2
  29.2 12.3 %copy-start.6 = (bf16[512]{0:T(512)(128)(2,1)S(1)}, bf16[512]{0:T(512)(128)(2,1)}, u32[]{:S(2)}) copy-start(bf16[512]{0:T(512)(128)(2,1)} %param.24) | copy-start | bytes 3076
  30.2 31.4 %copy-start.7 = (bf16[512]{0:T(512)(128)(2,1)S(1)}, bf16[512]{0:T(512)(128)(2,1)}, u32[]{:S(2)}) copy-start(bf16[512]{0:T(512)(128)(2,1)} %param.27) | copy-start | bytes 3076
  30.2 31.4 %copy-start.5 = (bf16[2048]{0:T(1024)(128)(2,1)S(1)}, bf16[2048]{0:T(1024)(128)(2,1)}, u32[]{:S(2)}) copy-start(bf16[2048]{0:T(1024)(128)(2,1)} %param.30) | copy-start | bytes 12292
  30.5 11.0 %collective-permute-start = (bf16[2,6,12,512]{3,2,1,0:T(8,128)(2,1)S(1)}, bf16[2,6,12,512]{3,2,1,0:T(8,128)(2,1)S(1)}, u32[]{:S(2)}, u32[]{:S(2)}) collective-permute-start(bf16[2,6,12,512]{3,2,1,0:T(8,128)(2,1)S(1)} %fusion.54), channel_id=1, source_target_pairs={{0,64},{64,128},{128,192},{1,65},{65,129},{129,193},{2,66},{66,130... | collective-permute-start | bytes 442376 | tf_op jit(solution)/shard_map/ppermute | solution.py:24
  38.2 15.8 %collective-permute-start.1 = (bf16[2,6,12,512]{3,2,1,0:T(8,128)(2,1)S(1)}, bf16[2,6,12,512]{3,2,1,0:T(8,128)(2,1)S(1)}, u32[]{:S(2)}, u32[]{:S(2)}) collective-permute-start(bf16[2,6,12,512]{3,2,1,0:T(8,128)(2,1)S(1)} %fusion.54), channel_id=1, source_target_pairs={{64,0},{128,64},{192,128},{65,1},{129,65},{193,129},{66,2},{130,66... | collective-permute-start | bytes 442376 | tf_op jit(solution)/shard_map/ppermute | solution.py:27
  54.5 12.8 %collective-permute-start.2 = (bf16[2,18,12,512]{3,0,2,1:T(2,128)(2,1)S(1)}, bf16[2,18,12,512]{3,0,2,1:T(2,128)(2,1)}, u32[]{:S(2)}, u32[]{:S(2)}) collective-permute-start(bf16[2,18,12,512]{3,0,2,1:T(2,128)(2,1)S(1)} %copy.130), channel_id=1, source_target_pairs={{0,1},{1,2},{2,3},{3,4},{4,5},{5,6},{6,7},{7,8},{8,9},{9,10},{10,1... | collective-permute-start | bytes 1327112 | tf_op jit(solution)/shard_map/ppermute | solution.py:24
  54.7 13.6 %collective-permute-start.3 = (bf16[2,18,12,512]{3,0,2,1:T(2,128)(2,1)S(1)}, bf16[2,18,12,512]{3,0,2,1:T(2,128)(2,1)}, u32[]{:S(2)}, u32[]{:S(2)}) collective-permute-start(bf16[2,18,12,512]{3,0,2,1:T(2,128)(2,1)S(1)} %copy.130), channel_id=1, source_target_pairs={{1,0},{2,1},{3,2},{4,3},{5,4},{6,5},{7,6},{8,7},{9,8},{10,9},{11,1... | collective-permute-start | bytes 1327112 | tf_op jit(solution)/shard_map/ppermute | solution.py:27
  69.5 1.8 %copy-start.8 = (bf16[512,1536]{1,0:T(8,128)(2,1)S(1)}, bf16[512,1536]{1,0:T(8,128)(2,1)}, u32[]{:S(2)}) copy-start(bf16[512,1536]{1,0:T(8,128)(2,1)} %param.25) | copy-start | bytes 4718596
  88.7 1.4 %copy-start.4 = (pred[4,144,144]{1,2,0:T(8,128)(4,1)S(1)}, pred[4,144,144]{1,2,0:T(8,128)(4,1)}, u32[]{:S(2)}) copy-start(pred[4,144,144]{1,2,0:T(8,128)(4,1)} %broadcast_compare_fusion) | copy-start | bytes 248836
  90.1 9.5 %copy-start.1 = (bf16[4,144,512]{1,2,0:T(8,128)(2,1)S(1)}, bf16[4,144,512]{1,2,0:T(8,128)(2,1)}, u32[]{:S(2)}) copy-start(bf16[4,144,512]{1,2,0:T(8,128)(2,1)} %copy.136) | copy-start | bytes 1769476
  109.6 5.0 %copy-start.3 = (bf16[512,512]{1,0:T(8,128)(2,1)S(1)}, bf16[512,512]{1,0:T(8,128)(2,1)}, u32[]{:S(2)}) copy-start(bf16[512,512]{1,0:T(8,128)(2,1)} %param.26) | copy-start | bytes 1572868
where the time goes:
time: 124 us
  local copies, waits for them, and re-layouts  41.5 us (33%)
  matrix products  33.4 us (27%)
  starting transfers between devices  20 us (16%)
  waiting for transfers between devices  19.9 us (16%)
  other arithmetic  6.8 us (5%)
  between operations  1.82 us (1%)
    ppermute x2, waiting for transfers between devices, extended(): lax.ppermute(lax.slice_in_dim(block, 0, width, axis=dim), axis, backward)  12.4 us
    dot_general x6, matrix products, project(): product = jnp.dot(flat_rows, weight, preferred_element_type=jnp.float32)  9.6 us
    sub x1, matrix products, on_device(): weights = jax.nn.softmax(scores, axis=-1).astype(jnp.bfloat16)  9.45 us
    ppermute x2, starting transfers between devices, extended(): lax.ppermute(lax.slice_in_dim(block, 0, width, axis=dim), axis, backward)  8.59 us
    ppermute x2, starting transfers between devices, extended(): lax.ppermute(lax.slice_in_dim(block, block.shape[dim] - width, None, axis...  7.93 us
    dot_general x1, matrix products, on_device(): jnp.einsum('whqk,wkhe->wqhe', weights, value_part, preferred_element_type...  5.43 us
    reshape x1, local copies, waits for them, and re-layouts, on_device(): blocked.transpose(1, 3, 0, 2, 4, 5)  5.16 us
    dot_general x1, matrix products, encode(): jnp.einsum('khe,lrche->rchkl', query_heads, key_part, preferred_element_t...  5.1 us
  transfers between devices with their start and end apart: 5, of which 3 were waited for; matrix products, arithmetic and copies ran while one was open for 4% of the time, Pallas kernels for 0%

commit v1 on v0

v1 whole, which is shorter than its diff:
```python
import math

import jax
import jax.numpy as jnp
from jax import lax
from jax.experimental import pallas as pl
from jax.experimental.pallas import tpu as pltpu
from jax.sharding import PartitionSpec as P

HEADS = 16
WH = 6
WW = 12
LATENT = 2
D = 512
HD = D // HEADS
TOK = LATENT * WH * WW
EPSILON = 1e-05
NEG_LARGE = -1e30
F32 = jnp.float32
BF16 = jnp.bfloat16
SCALE = 1.0 / math.sqrt(HD)
AXES = ("lat", "lon", "lev")


def layer_norm(values, gain_row):
    centre = values - jnp.mean(values, axis=-1, keepdims=True)
    spread = jnp.mean(centre * centre, axis=-1, keepdims=True)
    return centre * lax.rsqrt(spread + EPSILON) * gain_row


def dot(a, b):
    return jnp.dot(a, b, preferred_element_type=F32)


def dot_t(a, b):
    return lax.dot_general(a, b, (((1,), (1,)), ((), ())), preferred_element_type=F32)


def iota(shape, dim):
    return lax.broadcasted_iota(jnp.int32, shape, dim)


def split(index, size):
    whole = jnp.floor((index.astype(F32) + 0.5) * (1.0 / size)).astype(jnp.int32)
    return whole, index - whole * size


def token_coords(index):
    level, rest = split(index, WH * WW)
    row, col = split(rest, WW)
    return level, row, col


def level_keyval(levels_ref, gain_row, w_kv):
    pieces = [
        levels_ref[l, r].astype(F32)
        for l in range(levels_ref.shape[0])
        for r in range(levels_ref.shape[1])
    ]
    normed = layer_norm(jnp.concatenate(pieces, axis=0), gain_row).astype(BF16)
    return dot(normed, w_kv).astype(BF16)


def local_kernel(levels_ref, gain_ref, lq_ref, wq_ref, wkv_ref, score_ref, value_ref, query_ref):
    queries = dot(lq_ref[...], wq_ref[...]).astype(BF16).astype(F32)
    rows = LATENT * HEADS
    spread = jnp.concatenate(
        [jnp.broadcast_to(queries[k : k + 1], (HEADS, D)) for k in range(LATENT)], axis=0
    )
    head_of_row = split(iota((rows, 1), 0), HEADS)[1]
    head_of_lane = split(iota((1, D), 1), HD)[0]
    query_rows = jnp.where(head_of_row == head_of_lane, spread, 0.0).astype(BF16)
    keyval = level_keyval(levels_ref, gain_ref[...].astype(F32), wkv_ref[...])
    score_ref[...] = dot_t(keyval[:, :D], query_rows)
    value_ref[...] = keyval[:, D:]
    query_ref[...] = query_rows


def encode_kernel(
    levels_ref, score_ref, value_ref, query_ref, gain_ref, lq_ref, wkv_ref, wcross_ref,
    both_ref, own_ref, other_ref,
):
    lev = lax.axis_index("lev")
    keyval = level_keyval(levels_ref, gain_ref[...].astype(F32), wkv_ref[...])
    far_scores = dot_t(keyval[:, :D], query_ref[...])
    near_scores = score_ref[...]
    count = near_scores.shape[0] // 2
    scores = [s[i * count : (i + 1) * count] * SCALE for s in (near_scores, far_scores) for i in (0, 1)]
    top = jnp.maximum(jnp.maximum(scores[0], scores[1]), jnp.maximum(scores[2], scores[3]))
    powers = [jnp.exp(s - top) for s in scores]
    norm = 1.0 / (powers[0] + powers[1] + powers[2] + powers[3])
    weights = jnp.concatenate([p * norm for p in powers], axis=0).astype(BF16)
    lane = iota((1, LATENT * D), 1)
    expand = (iota((LATENT * HEADS, 1), 0) == split(lane, HD)[0]).astype(F32).astype(BF16)
    wide = dot(weights, expand)
    near_values = value_ref[...].astype(F32)
    far_values = keyval[:, D:].astype(F32)
    values = [x[i * count : (i + 1) * count] for x in (near_values, far_values) for i in (0, 1)]
    attended = []
    for k in range(LATENT):
        total = 0.0
        for l in range(4):
            total = total + wide[l * count : (l + 1) * count, k * D : (k + 1) * D] * values[l]
        attended.append(total.astype(BF16))
    projected = dot(jnp.concatenate(attended, axis=0), wcross_ref[...])
    query = lq_ref[...].astype(F32)
    latents = jnp.concatenate(
        [projected[k * count : (k + 1) * count] + query[k : k + 1] for k in range(LATENT)], axis=0
    ).astype(BF16)
    half, rest = split(iota((2 * TOK, 1), 0), TOK)
    level, row, col = token_coords(rest)
    side = jnp.where(half == 0, lev, 1 - lev)
    source = level * count + row * (2 * WW) + col + side * WW
    order = (iota((1, 2 * TOK), 1) == source).astype(F32).astype(BF16)
    both = dot(order, latents).astype(BF16)
    both_ref[...] = both
    own_ref[...] = both[:TOK]
    other_ref[...] = both[TOK:]


def block_kernel(
    shift_lat_ref, shift_lon_ref, both_ref, far_ref, chip_ref, chip_far_ref, cross_ref,
    cross_far_ref, attn_gain_ref, wqkv_ref, wproj_ref, mlp_gain_ref, wup_ref, wdown_ref,
    merge_gain_ref, wmerge_ref, out_ref,
):
    lat = lax.axis_index("lat")
    lev = lax.axis_index("lev")
    last_lat = lax.axis_size("lat") - 1
    shift_row = shift_lat_ref[0]
    shift_col = shift_lon_ref[0]
    _, row, col = token_coords(iota((TOK, 1), 0))
    row_low = (row >= WH - shift_row).astype(jnp.int32)
    col_low = (col >= WW - shift_col).astype(jnp.int32)
    use_other = col_low == lev
    use_chip = row_low == lat % 2
    own = both_ref[:TOK].astype(F32)
    other = both_ref[TOK:].astype(F32)
    chip_own = chip_ref[:TOK].astype(F32)
    chip_other = chip_ref[TOK:].astype(F32)
    cross_other = cross_ref[:TOK].astype(F32)
    cross_own = cross_ref[TOK:].astype(F32)
    far = far_ref[...].astype(F32)
    chip_far = chip_far_ref[...].astype(F32)
    cross_far = cross_far_ref[...].astype(F32)
    beside = jnp.where(use_other, other, far)
    above = jnp.where(use_chip, chip_own, cross_own)
    corner = jnp.where(
        use_chip, jnp.where(use_other, chip_other, chip_far), jnp.where(use_other, cross_other, cross_far)
    )
    tokens = jnp.concatenate([own, beside, above, corner], axis=0)
    normed = layer_norm(tokens, attn_gain_ref[...].astype(F32)).astype(BF16)
    query = dot(normed[:TOK], wqkv_ref[:, :D]).astype(BF16)
    keyval = dot(normed, wqkv_ref[:, D:]).astype(BF16)

    group, rest = split(iota((1, 4 * TOK), 1), TOK)
    _, key_row, key_col = token_coords(rest)
    group_row, group_col = split(group, 2)
    key_row_low = (key_row >= WH - shift_row).astype(jnp.int32)
    key_col_low = (key_col >= WW - shift_col).astype(jnp.int32)
    key_label = (key_row_low ^ group_row) * 2 + (key_col_low ^ group_col)
    outside = (group_row == 1) & (
        ((lat == 0) & (key_row_low == 1)) | ((lat == last_lat) & (key_row_low == 0))
    )
    key_label = jnp.where(outside, -1, key_label)
    bias = jnp.where(row_low * 2 + col_low == key_label, 0.0, NEG_LARGE)

    lanes = 256
    per = lanes // HD
    head_of_lane = split(iota((1, lanes), 1), HD)[0]
    window_parts = []
    for g in range(D // lanes):
        query_g = query[:, g * lanes : (g + 1) * lanes]
        key_g = keyval[:, g * lanes : (g + 1) * lanes]
        value_g = keyval[:, D + g * lanes : D + (g + 1) * lanes]
        total = jnp.zeros((TOK, lanes), F32)
        for h in range(per):
            here = head_of_lane == h
            scores = dot_t(query_g * here.astype(F32).astype(BF16), key_g) * SCALE + bias
            powers = jnp.exp(scores - jnp.max(scores, axis=-1, keepdims=True))
            weights = (powers * (1.0 / jnp.sum(powers, axis=-1, keepdims=True))).astype(BF16)
            total = jnp.where(here, dot(weights, value_g), total)
        window_parts.append(total.astype(BF16))
    window_out = jnp.concatenate(window_parts, axis=1)

    middle = own + dot(window_out, wproj_ref[...])
    mlp_in = layer_norm(middle, mlp_gain_ref[...].astype(F32)).astype(BF16)
    up = dot(mlp_in, wup_ref[...])
    inner = math.sqrt(2.0 / math.pi) * (up + 0.044715 * (up * up * up))
    hidden = (0.5 * up * (1.0 + jnp.tanh(inner))).astype(BF16)
    block_out = (middle + dot(hidden, wdown_ref[...])).astype(BF16)

    groups = LATENT * WH // 2
    rows = 8 * groups
    corner_index, place = split(iota((4 * rows, 1), 0), rows)
    pair, col_pair = split(place, 8)
    level, row_pair = split(pair, WH // 2)
    corner_col, corner_row = split(corner_index, 2)
    source = level * (WH * WW) + (row_pair * 2 + corner_row) * WW + col_pair * 2 + corner_col
    source = jnp.where(col_pair < WW // 2, source, -1)
    order = (iota((1, TOK), 1) == source).astype(F32).astype(BF16)
    sorted_out = dot(order, block_out)
    grouped = jnp.concatenate([sorted_out[i * rows : (i + 1) * rows] for i in range(4)], axis=1)
    merge_in = layer_norm(grouped, merge_gain_ref[...].astype(F32)).astype(BF16)
    merged = dot(merge_in, wmerge_ref[...])
    for k in range(LATENT):
        for i in range(WH // 2):
            start = (k * (WH // 2) + i) * 8
            out_ref[k, i] = merged[start : start + WW // 2].astype(BF16)


VMEM_SPEC = pl.BlockSpec(memory_space=pltpu.VMEM)
SMEM_SPEC = pl.BlockSpec(memory_space=pltpu.SMEM)


def params(mib):
    return pltpu.CompilerParams(vmem_limit_bytes=mib * 2**20)


def pairs(lats, lons, target):
    chosen = []
    for lat in range(lats):
        for lon in range(lons):
            for lev in range(2):
                to_lat, to_lon, to_lev = target(lat, lon, lev)
                chosen.append(
                    ((lat * lons + lon) * 2 + lev, (to_lat * lons + to_lon % lons) * 2 + to_lev)
                )
    return chosen


def on_device(
    levels_in,
    enc_gain,
    latent_query,
    w_query,
    w_kv,
    w_cross_out,
    shift_lat,
    shift_lon,
    attn_gain,
    w_qkv,
    w_proj,
    mlp_gain,
    w_up,
    w_down,
    merge_gain,
    w_merge,
):
    lats = lax.axis_size("lat")
    lons = lax.axis_size("lon")

    def chip(lat):
        return lat ^ 1

    def cross(lat):
        return (lat + 1) % lats if lat % 2 else (lat - 1) % lats

    def aside(lon, lev):
        return (lon - 1, 1) if lev == 0 else (lon + 1, 0)

    level_pairs = pairs(lats, lons, lambda a, o, v: (a, o, 1 - v))
    far_pairs = pairs(lats, lons, lambda a, o, v: (a, o + 1 if v == 0 else o - 1, v))
    chip_pairs = pairs(lats, lons, lambda a, o, v: (chip(a), o, v))
    cross_pairs = pairs(lats, lons, lambda a, o, v: (cross(a), o, 1 - v))
    corner_pairs = pairs(lats, lons, lambda a, o, v: (cross(a),) + aside(o, v))

    enc_row = enc_gain.reshape(1, D)
    far_levels = lax.ppermute(levels_in, AXES, level_pairs)
    positions = levels_in.shape[0] * levels_in.shape[1] * levels_in.shape[2]
    scores, values, query_rows = pl.pallas_call(
        local_kernel,
        out_shape=(
            jax.ShapeDtypeStruct((positions, LATENT * HEADS), F32),
            jax.ShapeDtypeStruct((positions, D), BF16),
            jax.ShapeDtypeStruct((LATENT * HEADS, D), BF16),
        ),
        in_specs=[VMEM_SPEC] * 5,
        out_specs=(VMEM_SPEC,) * 3,
        compiler_params=params(24),
        name="local_levels",
    )(levels_in, enc_row, latent_query, w_query, w_kv)
    both, own, other = pl.pallas_call(
        encode_kernel,
        out_shape=(
            jax.ShapeDtypeStruct((2 * TOK, D), BF16),
            jax.ShapeDtypeStruct((TOK, D), BF16),
            jax.ShapeDtypeStruct((TOK, D), BF16),
        ),
        in_specs=[VMEM_SPEC] * 8,
        out_specs=(VMEM_SPEC,) * 3,
        compiler_params=params(24),
        name="encode",
    )(far_levels, scores, values, query_rows, enc_row, latent_query, w_kv, w_cross_out)
    far = lax.ppermute(other, AXES, far_pairs)
    cross_far = lax.ppermute(own, AXES, corner_pairs)
    cross_both = lax.ppermute(both, AXES, cross_pairs)
    chip_both = lax.ppermute(both, AXES, chip_pairs)
    chip_far = lax.ppermute(far, AXES, chip_pairs)
    return pl.pallas_call(
        block_kernel,
        out_shape=jax.ShapeDtypeStruct((LATENT, WH // 2, WW // 2, w_merge.shape[1]), BF16),
        in_specs=[SMEM_SPEC] * 2 + [VMEM_SPEC] * 14,
        out_specs=VMEM_SPEC,
        compiler_params=params(48),
        name="window_block",
    )(
        shift_lat, shift_lon, both, far, chip_both, chip_far, cross_both, cross_far,
        attn_gain.reshape(1, D), w_qkv, w_proj, mlp_gain.reshape(1, D), w_up, w_down,
        merge_gain.reshape(1, 4 * D), w_merge,
    )


def solution(mesh):
    in_specs = (P("lev", "lat", "lon", None),) + (P(),) * 15
    out_specs = P(None, "lat", ("lon", "lev"), None)
    return jax.shard_map(
        on_device, mesh=mesh, in_specs=in_specs, out_specs=out_specs, check_vma=False
    )
```

time: 124 us -> 51.5 us (0.42)
  local copies, waits for them, and re-layouts: 41.5 us -> 7.85 us
  matrix products: 33.4 us -> 0 us
  Pallas kernels: 0 us -> 16 us
  waiting for transfers between devices: 19.9 us -> 9.59 us
  other arithmetic: 6.8 us -> 0 us
  starting transfers between devices: 20 us -> 16.3 us
    dot_general x10 -> x0, matrix products: 24 us -> none  [the longest x6 9.6 us: project(): product = jnp.dot(flat_rows, weight, preferred_element_type=jnp.float32)]
    pallas_call x0 -> x3, Pallas kernels: none -> 16 us  [the longest x1 13.4 us: on_device(): pl.pallas_call(block_kernel, out_shape=jax.ShapeDtypeStruct((LATENT, WH /...]
    reshape x5 -> x4, local copies, waits for them, and re-layouts: 12.9 us -> 0.73 us  [the longest x1 0.71 us: on_device(): enc_row = enc_gain.reshape(1, D)]
    sub x1 -> x0, matrix products: 9.45 us -> none  [on_device(): weights = jax.nn.softmax(scores, axis=-1).astype(jnp.bfloat16)]
    convert_element_type x9 -> x0, local copies, waits for them, and re-layouts: 9.01 us -> none  [the longest x1 4.61 us: on_device(): window_out.astype(jnp.bfloat16)]
    slice x5 -> x0, local copies, waits for them, and re-layouts: 8.01 us -> none  [the longest x2 4.28 us: on_device(): blocked[..., feat_width:2 * feat_width]]
    ppermute x4 -> x6, waiting for transfers between devices: 17.2 us -> 9.59 us  [the longest x1 9.18 us: on_device(): cross_far = lax.ppermute(own, AXES, corner_pairs)]
    unnamed x19 -> x24, local copies, waits for them, and re-layouts: 2.35 us -> 6.42 us
  transfers between devices with their start and end apart: 5 -> 6, of which waited for: 3 -> 2; matrix products, arithmetic and copies ran while one was open for 4% -> 1% of each run, Pallas kernels for 0% -> 2%
where the time goes in v1:
time: 51.5 us; the launch traced here: 51.2 us
  starting transfers between devices  16.3 us (32%)
  Pallas kernels  16 us (31%)
  waiting for transfers between devices  9.59 us (19%)
  local copies, waits for them, and re-layouts  7.85 us (15%)
  between operations  1.41 us (3%)
    pallas_call x1, Pallas kernels, on_device(): pl.pallas_call(block_kernel, out_shape=jax.ShapeDtypeStruct((LATENT, WH /...  13.4 us
    ppermute x1, starting transfers between devices, on_device(): cross_both = lax.ppermute(both, AXES, cross_pairs)  10.6 us
    ppermute x1, waiting for transfers between devices, on_device(): cross_far = lax.ppermute(own, AXES, corner_pairs)  9.18 us
    unnamed x24, local copies, waits for them, and re-layouts  6.42 us
    ppermute x1, starting transfers between devices, on_device(): far = lax.ppermute(other, AXES, far_pairs)  2.66 us
    ppermute x1, starting transfers between devices, on_device(): far_levels = lax.ppermute(levels_in, AXES, level_pairs)  2.13 us
    pallas_call x1, Pallas kernels, on_device(): pl.pallas_call(encode_kernel, out_shape=(jax.ShapeDtypeStruct((2 * TOK, D...  1.83 us
  transfers between devices with their start and end apart: 6, of which 2 were waited for; matrix products, arithmetic and copies ran while one was open for 1% of the time, Pallas kernels for 2%

profile of v1, /device:TPU:1, one launch (start us, length us, event | category | flops | bytes accessed | tf_op | source)
XLA Modules:
  0.0 51.2 jit_solution(18436046834481259356)
XLA Ops:
  0.0 2.1 %collective-permute-start = (bf16[2,6,24,512]{3,2,1,0:T(8,128)(2,1)}, bf16[2,6,24,512]{3,2,1,0:T(8,128)(2,1)S(1)}, u32[]{:S(2)}, u32[]{:S(2)}) collective-permute-start(bf16[2,6,24,512]{3,2,1,0:T(8,128)(2,1)} %levels_ref.1), channel_id=1, source_target_pairs={{0,1},{1,0},{2,3},{3,2},{4,5},{5,4},{6,7},{7,6},{8,9},{9,8},{10,11... | collective-permute-start | bytes 884744 | tf_op jit(solution)/shard_map/ppermute | solution.py:268
  2.1 0.0 copy-start.10
  2.1 0.0 copy-start.11
  2.1 0.7 %reshape.12.gain_ref = bf16[1,512]{1,0:T(2,128)(2,1)S(1)} reshape(bf16[512]{0:T(512)(128)(2,1)} %param.17) | data formatting | bytes 2048 | tf_op jit(solution)/shard_map/reshape | solution.py:267
  2.8 0.0 copy-start
  2.8 1.2 %copy-done = bf16[512,1024]{1,0:T(8,128)(2,1)S(1)} copy-done((bf16[512,1024]{1,0:T(8,128)(2,1)S(1)}, bf16[512,1024]{1,0:T(8,128)(2,1)}, u32[]{:S(2)}) %copy-start) | copy-done | bytes 1048600
  4.1 0.0 copy-start.4
  4.1 1.0 %copy-done.4 = bf16[512,512]{1,0:T(8,128)(2,1)S(1)} copy-done((bf16[512,512]{1,0:T(8,128)(2,1)S(1)}, bf16[512,512]{1,0:T(8,128)(2,1)}, u32[]{:S(2)}) %copy-start.4) | copy-done | bytes 524312
  5.1 0.0 copy-start.7
  5.1 1.0 %copy-done.7 = bf16[2,6,24,512]{3,2,1,0:T(8,128)(2,1)S(1)} copy-done((bf16[2,6,24,512]{3,2,1,0:T(8,128)(2,1)S(1)}, bf16[2,6,24,512]{3,2,1,0:T(8,128)(2,1)}, u32[]{:S(2)}) %copy-start.7) | copy-done | bytes 294936
  6.1 0.0 copy-start.8
  6.1 0.7 %copy-done.8 = bf16[2,512]{1,0:T(2,128)(2,1)S(1)} copy-done((bf16[2,512]{1,0:T(2,128)(2,1)S(1)}, bf16[2,512]{1,0:T(2,128)(2,1)}, u32[]{:S(2)}) %copy-start.8) | copy-done | bytes 2072
  6.8 0.0 copy-start.1
  6.8 0.0 copy-start.2
  6.8 0.0 copy-start.5
  6.8 0.8 %local_levels.1 = (f32[288,32]{1,0:T(8,128)S(1)}, bf16[288,512]{1,0:T(8,128)(2,1)S(1)}, bf16[32,512]{1,0:T(8,128)(2,1)S(1)}) custom-call(bf16[2,6,24,512]{3,2,1,0:T(8,128)(2,1)S(1)} %copy-done.7, bf16[1,512]{1,0:T(2,128)(2,1)S(1)} %reshape.12.gain_ref, bf16[2,512]{1,0:T(2,128)(2,1)S(1)} %copy-done.8, bf16[512,512]{1,0:T(8,128)(2,1)S(1)} %copy-done.4, ...), custom_call_target="tpu_custom_call" | custom-call | tf_op jit(solution)/shard_map/local_levels/pallas_call | solution.py:270
  7.5 0.4 collective-permute-done.levels_ref
  7.9 0.0 copy-done.1
  8.0 0.0 copy-start.6
  8.0 1.0 %copy-done.6 = bf16[512,512]{1,0:T(8,128)(2,1)S(1)} copy-done((bf16[512,512]{1,0:T(8,128)(2,1)S(1)}, bf16[512,512]{1,0:T(8,128)(2,1)}, u32[]{:S(2)}) %copy-start.6) | copy-done | bytes 524312
  9.0 0.0 copy-start.9
  9.0 1.8 %encode.1 = (bf16[288,512]{1,0:T(8,128)(2,1)S(1)}, bf16[144,512]{1,0:T(8,128)(2,1)S(1)}, bf16[144,512]{1,0:T(8,128)(2,1)S(1)}) custom-call(bf16[2,6,24,512]{3,2,1,0:T(8,128)(2,1)S(1)} %collective-permute-done.levels_ref, f32[288,32]{1,0:T(8,128)S(1)} %get-tuple-element.11.score_ref, bf16[288,512]{1,0:T(8,128)(2,1)S(1)} %get-tuple-element.12.value_ref, ...), custom_call_target="tpu_custom_call" | custom-call | tf_op jit(solution)/shard_map/encode/pallas_call | solution.py:282
  10.9 2.7 %collective-permute-start.1 = (bf16[144,512]{1,0:T(8,128)(2,1)S(1)}, bf16[144,512]{1,0:T(8,128)(2,1)S(1)}, u32[]{:S(2)}, u32[]{:S(2)}) collective-permute-start(bf16[144,512]{1,0:T(8,128)(2,1)S(1)} %get-tuple-element.15), channel_id=1, source_target_pairs={{0,2},{1,63},{2,4},{3,1},{4,6},{5,3},{6,8},{7,5},{8,10},{9,7},{10,... | collective-permute-start | bytes 442376 | tf_op jit(solution)/shard_map/ppermute | solution.py:294
  13.5 10.6 %collective-permute-start.4 = (bf16[288,512]{1,0:T(8,128)(2,1)S(1)}, bf16[288,512]{1,0:T(8,128)(2,1)S(1)}, u32[]{:S(2)}, u32[]{:S(2)}) collective-permute-start(bf16[288,512]{1,0:T(8,128)(2,1)S(1)} %get-tuple-element.14.both_ref), channel_id=1, source_target_pairs={{0,193},{1,192},{2,195},{3,194},{4,197},{5,196},{6,199},{7,198},{8... | collective-permute-start | bytes 884744 | tf_op jit(solution)/shard_map/ppermute | solution.py:296
  24.1 0.0 collective-permute-start.2
  24.1 0.4 collective-permute-start.5
  24.5 0.0 collective-permute-done.1.far_ref
  24.5 0.5 collective-permute-start.3
  26.4 0.0 copy-done.10
  26.4 0.0 copy-done.11
  26.4 0.0 copy-done.9
  26.4 9.2 %collective-permute-done.5.cross_far_ref = bf16[144,512]{1,0:T(8,128)(2,1)S(1)} collective-permute-done((bf16[144,512]{1,0:T(8,128)(2,1)S(1)}, bf16[144,512]{1,0:T(8,128)(2,1)S(1)}, u32[]{:S(2)}, u32[]{:S(2)}) %collective-permute-start.5) | collective-permute-done | bytes 147488 | tf_op jit(solution)/shard_map/ppermute | solution.py:295
  35.6 0.0 collective-permute-done.3.chip_far_ref
  35.6 0.0 collective-permute-done.4.cross_ref
  35.6 0.0 collective-permute-done.2.chip_ref
  35.6 0.0 copy-done.2
  35.6 0.0 copy-done.5
  35.6 0.0 copy-start.3
  35.7 1.4 %copy-done.3 = bf16[512,1536]{1,0:T(8,128)(2,1)S(1)} copy-done((bf16[512,1536]{1,0:T(8,128)(2,1)S(1)}, bf16[512,1536]{1,0:T(8,128)(2,1)}, u32[]{:S(2)}) %copy-start.3) | copy-done | bytes 1572888
  37.1 13.4 %window_block.1 = bf16[2,3,6,1024]{3,2,1,0:T(8,128)(2,1)S(1)} custom-call(s32[1]{0:T(128)S(6)} %copy.18.shift_lat_ref, s32[1]{0:T(128)S(6)} %copy.19.shift_lon_ref, bf16[288,512]{1,0:T(8,128)(2,1)S(1)} %get-tuple-element.14.both_ref, bf16[144,512]{1,0:T(8,128)(2,1)S(1)} %collective-permute-done.1.far_ref, ...), custom_call_target="tpu_custom_call" | custom-call | tf_op jit(solution)/shard_map/window_block/pallas_call | solution.py:299
  50.5 0.7 %copy.17 = bf16[2,3,6,1024]{3,0,2,1:T(2,128)(2,1)} copy(bf16[2,3,6,1024]{3,2,1,0:T(8,128)(2,1)S(1)} %window_block.1) | data formatting | bytes 147456 | tf_op jit(solution)/shard_map/window_block/pallas_call | solution.py:299
  (3 shorter events, 0.0 us)
Async XLA Ops:
  0.0 7.9 %collective-permute-start = (bf16[2,6,24,512]{3,2,1,0:T(8,128)(2,1)}, bf16[2,6,24,512]{3,2,1,0:T(8,128)(2,1)S(1)}, u32[]{:S(2)}, u32[]{:S(2)}) collective-permute-start(bf16[2,6,24,512]{3,2,1,0:T(8,128)(2,1)} %levels_ref.1), channel_id=1, source_target_pairs={{0,1},{1,0},{2,3},{3,2},{4,5},{5,4},{6,7},{7,6},{8,9},{9,8},{10,11... | collective-permute-start | bytes 884744 | tf_op jit(solution)/shard_map/ppermute | solution.py:268
  2.1 24.2 %copy-start.10 = (bf16[512]{0:T(512)(128)(2,1)S(1)}, bf16[512]{0:T(512)(128)(2,1)}, u32[]{:S(2)}) copy-start(bf16[512]{0:T(512)(128)(2,1)} %param.24) | copy-start | bytes 3076
  2.1 24.2 %copy-start.11 = (bf16[512]{0:T(512)(128)(2,1)S(1)}, bf16[512]{0:T(512)(128)(2,1)}, u32[]{:S(2)}) copy-start(bf16[512]{0:T(512)(128)(2,1)} %param.27) | copy-start | bytes 3076
  2.8 1.2 %copy-start = (bf16[512,1024]{1,0:T(8,128)(2,1)S(1)}, bf16[512,1024]{1,0:T(8,128)(2,1)}, u32[]{:S(2)}) copy-start(bf16[512,1024]{1,0:T(8,128)(2,1)} %wkv_ref.3) | copy-start | bytes 3145732
  4.1 1.0 %copy-start.4 = (bf16[512,512]{1,0:T(8,128)(2,1)S(1)}, bf16[512,512]{1,0:T(8,128)(2,1)}, u32[]{:S(2)}) copy-start(bf16[512,512]{1,0:T(8,128)(2,1)} %wq_ref.1) | copy-start | bytes 1572868
  5.1 1.0 %copy-start.7 = (bf16[2,6,24,512]{3,2,1,0:T(8,128)(2,1)S(1)}, bf16[2,6,24,512]{3,2,1,0:T(8,128)(2,1)}, u32[]{:S(2)}) copy-start(bf16[2,6,24,512]{3,2,1,0:T(8,128)(2,1)} %levels_ref.1) | copy-start | bytes 884740
  6.1 0.7 %copy-start.8 = (bf16[2,512]{1,0:T(2,128)(2,1)S(1)}, bf16[2,512]{1,0:T(2,128)(2,1)}, u32[]{:S(2)}) copy-start(bf16[2,512]{1,0:T(2,128)(2,1)} %lq_ref.3) | copy-start | bytes 6148
  6.8 1.2 %copy-start.1 = (bf16[512,1024]{1,0:T(8,128)(2,1)S(1)}, bf16[512,1024]{1,0:T(8,128)(2,1)}, u32[]{:S(2)}) copy-start(bf16[512,1024]{1,0:T(8,128)(2,1)} %wkv_ref.3) | copy-start | bytes 3145732
  6.8 28.9 %copy-start.2 = (bf16[512,2048]{1,0:T(8,128)(2,1)S(1)}, bf16[512,2048]{1,0:T(8,128)(2,1)}, u32[]{:S(2)}) copy-start(bf16[512,2048]{1,0:T(8,128)(2,1)} %wup_ref.1) | copy-start | bytes 6291460
  6.8 28.9 %copy-start.5 = (bf16[512,512]{1,0:T(8,128)(2,1)S(1)}, bf16[512,512]{1,0:T(8,128)(2,1)}, u32[]{:S(2)}) copy-start(bf16[512,512]{1,0:T(8,128)(2,1)} %wproj_ref.1) | copy-start | bytes 1572868
  8.0 1.0 %copy-start.6 = (bf16[512,512]{1,0:T(8,128)(2,1)S(1)}, bf16[512,512]{1,0:T(8,128)(2,1)}, u32[]{:S(2)}) copy-start(bf16[512,512]{1,0:T(8,128)(2,1)} %wcross_ref.1) | copy-start | bytes 1572868
  9.0 17.4 %copy-start.9 = (bf16[2048]{0:T(1024)(128)(2,1)S(1)}, bf16[2048]{0:T(1024)(128)(2,1)}, u32[]{:S(2)}) copy-start(bf16[2048]{0:T(1024)(128)(2,1)} %param.30) | copy-start | bytes 12292
  10.9 13.7 %collective-permute-start.1 = (bf16[144,512]{1,0:T(8,128)(2,1)S(1)}, bf16[144,512]{1,0:T(8,128)(2,1)S(1)}, u32[]{:S(2)}, u32[]{:S(2)}) collective-permute-start(bf16[144,512]{1,0:T(8,128)(2,1)S(1)} %get-tuple-element.15), channel_id=1, source_target_pairs={{0,2},{1,63},{2,4},{3,1},{4,6},{5,3},{6,8},{7,5},{8,10},{9,7},{10,... | collective-permute-start | bytes 442376 | tf_op jit(solution)/shard_map/ppermute | solution.py:294
  13.5 22.1 %collective-permute-start.4 = (bf16[288,512]{1,0:T(8,128)(2,1)S(1)}, bf16[288,512]{1,0:T(8,128)(2,1)S(1)}, u32[]{:S(2)}, u32[]{:S(2)}) collective-permute-start(bf16[288,512]{1,0:T(8,128)(2,1)S(1)} %get-tuple-element.14.both_ref), channel_id=1, source_target_pairs={{0,193},{1,192},{2,195},{3,194},{4,197},{5,196},{6,199},{7,198},{8... | collective-permute-start | bytes 884744 | tf_op jit(solution)/shard_map/ppermute | solution.py:296
  24.1 11.5 %collective-permute-start.2 = (bf16[288,512]{1,0:T(8,128)(2,1)S(1)}, bf16[288,512]{1,0:T(8,128)(2,1)S(1)}, u32[]{:S(2)}, u32[]{:S(2)}) collective-permute-start(bf16[288,512]{1,0:T(8,128)(2,1)S(1)} %get-tuple-element.14.both_ref), channel_id=1, source_target_pairs={{0,64},{1,65},{2,66},{3,67},{4,68},{5,69},{6,70},{7,71},{8,72},{9,... | collective-permute-start | bytes 884744 | tf_op jit(solution)/shard_map/ppermute | solution.py:297
  24.1 11.5 %collective-permute-start.5 = (bf16[144,512]{1,0:T(8,128)(2,1)S(1)}, bf16[144,512]{1,0:T(8,128)(2,1)S(1)}, u32[]{:S(2)}, u32[]{:S(2)}) collective-permute-start(bf16[144,512]{1,0:T(8,128)(2,1)S(1)} %get-tuple-element.16), channel_id=1, source_target_pairs={{0,255},{1,194},{2,193},{3,196},{4,195},{5,198},{6,197},{7,200},{8... | collective-permute-start | bytes 442376 | tf_op jit(solution)/shard_map/ppermute | solution.py:295
  24.5 11.1 %collective-permute-start.3 = (bf16[144,512]{1,0:T(8,128)(2,1)S(1)}, bf16[144,512]{1,0:T(8,128)(2,1)S(1)}, u32[]{:S(2)}, u32[]{:S(2)}) collective-permute-start(bf16[144,512]{1,0:T(8,128)(2,1)S(1)} %collective-permute-done.1.far_ref), channel_id=1, source_target_pairs={{0,64},{1,65},{2,66},{3,67},{4,68},{5,69},{6,70},{7,71},{8,72},{9,... | collective-permute-start | bytes 442376 | tf_op jit(solution)/shard_map/ppermute | solution.py:298
  35.6 1.4 %copy-start.3 = (bf16[512,1536]{1,0:T(8,128)(2,1)S(1)}, bf16[512,1536]{1,0:T(8,128)(2,1)}, u32[]{:S(2)}) copy-start(bf16[512,1536]{1,0:T(8,128)(2,1)} %wqkv_ref.1) | copy-start | bytes 4718596

commit v2 on v1

--- a/solution.py
+++ b/solution.py
@@ -19,6 +19,7 @@
 F32 = jnp.float32
 BF16 = jnp.bfloat16
 SCALE = 1.0 / math.sqrt(HD)
+LOG2E = math.log2(math.e)
 AXES = ("lat", "lon", "lev")
 
 
@@ -49,6 +50,10 @@
     level, rest = split(index, WH * WW)
     row, col = split(rest, WW)
     return level, row, col
+
+
+def row_of(ref):
+    return ref[...].astype(F32).reshape(1, ref.shape[0])
 
 
 def level_keyval(levels_ref, gain_row, w_kv):
@@ -61,7 +66,35 @@
     return dot(normed, w_kv).astype(BF16)
 
 
-def local_kernel(levels_ref, gain_ref, lq_ref, wq_ref, wkv_ref, score_ref, value_ref, query_ref):
+def local_kernel(
+    levels_hbm, gain_ref, lq_ref, wq_hbm, wkv_hbm, wqkv_hbm, wcross_hbm, wproj_hbm, wup_hbm,
+    wdown_hbm, wmerge_hbm,
+    score_ref, value_ref, query_ref, wq_t_ref, wv_t_ref, wk_ref, wkv_ref, wcross_ref, wproj_ref,
+    wup_ref, wdown_ref, wmerge_ref,
+    levels_ref, wq_ref, wqkv_ref, sems,
+):
+    moves = [
+        (levels_hbm, levels_ref),
+        (wkv_hbm, wkv_ref),
+        (wq_hbm, wq_ref),
+        (wqkv_hbm, wqkv_ref),
+        (wcross_hbm, wcross_ref),
+        (wproj_hbm, wproj_ref),
+        (wup_hbm, wup_ref),
+        (wdown_hbm, wdown_ref),
+        (wmerge_hbm, wmerge_ref),
+    ]
+    copies = [
+        pltpu.make_async_copy(source, target, sems.at[i])
+        for i, (source, target) in enumerate(moves)
+    ]
+    for copy in copies:
+        copy.start()
+    copies[0].wait()
+    copies[1].wait()
+    keyval = level_keyval(levels_ref, row_of(gain_ref), wkv_ref[...])
+    value_ref[...] = keyval[:, D:]
+    copies[2].wait()
     queries = dot(lq_ref[...], wq_ref[...]).astype(BF16).astype(F32)
     rows = LATENT * HEADS
     spread = jnp.concatenate(
@@ -70,10 +103,14 @@
     head_of_row = split(iota((rows, 1), 0), HEADS)[1]
     head_of_lane = split(iota((1, D), 1), HD)[0]
     query_rows = jnp.where(head_of_row == head_of_lane, spread, 0.0).astype(BF16)
-    keyval = level_keyval(levels_ref, gain_ref[...].astype(F32), wkv_ref[...])
     score_ref[...] = dot_t(keyval[:, :D], query_rows)
-    value_ref[...] = keyval[:, D:]
     query_ref[...] = query_rows
+    copies[3].wait()
+    wq_t_ref[...] = wqkv_ref[:, :D].astype(F32).T.astype(BF16)
+    wk_ref[...] = wqkv_ref[:, D : 2 * D]
+    wv_t_ref[...] = wqkv_ref[:, 2 * D :].astype(F32).T.astype(BF16)
+    for copy in copies[4:]:
+        copy.wait()
 
 
 def encode_kernel(
@@ -81,7 +118,7 @@
     both_ref, own_ref, other_ref,
 ):
     lev = lax.axis_index("lev")
-    keyval = level_keyval(levels_ref, gain_ref[...].astype(F32), wkv_ref[...])
+    keyval = level_keyval(levels_ref, row_of(gain_ref), wkv_ref[...])
     far_scores = dot_t(keyval[:, :D], query_ref[...])
     near_scores = score_ref[...]
     count = near_scores.shape[0] // 2
@@ -120,8 +157,8 @@
 
 def block_kernel(
     shift_lat_ref, shift_lon_ref, both_ref, far_ref, chip_ref, chip_far_ref, cross_ref,
-    cross_far_ref, attn_gain_ref, wqkv_ref, wproj_ref, mlp_gain_ref, wup_ref, wdown_ref,
-    merge_gain_ref, wmerge_ref, out_ref,
+    cross_far_ref, attn_gain_ref, wk_ref, wq_t_ref, wv_t_ref, wproj_ref, mlp_gain_ref, wup_ref,
+    wdown_ref, merge_gain_ref, wmerge_ref, out_ref,
 ):
     lat = lax.axis_index("lat")
     lev = lax.axis_index("lev")
@@ -133,83 +170,126 @@
     col_low = (col >= WW - shift_col).astype(jnp.int32)
     use_other = col_low == lev
     use_chip = row_low == lat % 2
+    gain = row_of(attn_gain_ref)
     own = both_ref[:TOK].astype(F32)
     other = both_ref[TOK:].astype(F32)
     chip_own = chip_ref[:TOK].astype(F32)
     chip_other = chip_ref[TOK:].astype(F32)
     cross_other = cross_ref[:TOK].astype(F32)
     cross_own = cross_ref[TOK:].astype(F32)
-    far = far_ref[...].astype(F32)
-    chip_far = chip_far_ref[...].astype(F32)
-    cross_far = cross_far_ref[...].astype(F32)
-    beside = jnp.where(use_other, other, far)
+    beside = jnp.where(use_other, other, far_ref[...].astype(F32))
     above = jnp.where(use_chip, chip_own, cross_own)
     corner = jnp.where(
-        use_chip, jnp.where(use_other, chip_other, chip_far), jnp.where(use_other, cross_other, cross_far)
-    )
-    tokens = jnp.concatenate([own, beside, above, corner], axis=0)
-    normed = layer_norm(tokens, attn_gain_ref[...].astype(F32)).astype(BF16)
-    query = dot(normed[:TOK], wqkv_ref[:, :D]).astype(BF16)
-    keyval = dot(normed, wqkv_ref[:, D:]).astype(BF16)
-
-    group, rest = split(iota((1, 4 * TOK), 1), TOK)
-    _, key_row, key_col = token_coords(rest)
-    group_row, group_col = split(group, 2)
-    key_row_low = (key_row >= WH - shift_row).astype(jnp.int32)
-    key_col_low = (key_col >= WW - shift_col).astype(jnp.int32)
-    key_label = (key_row_low ^ group_row) * 2 + (key_col_low ^ group_col)
-    outside = (group_row == 1) & (
-        ((lat == 0) & (key_row_low == 1)) | ((lat == last_lat) & (key_row_low == 0))
-    )
-    key_label = jnp.where(outside, -1, key_label)
-    bias = jnp.where(row_low * 2 + col_low == key_label, 0.0, NEG_LARGE)
+        use_chip,
+        jnp.where(use_other, chip_other, chip_far_ref[...].astype(F32)),
+        jnp.where(use_other, cross_other, cross_far_ref[...].astype(F32)),
+    )
+    own_n, beside_n, above_n, corner_n = [
+        layer_norm(x, gain) for x in (own, beside, above, corner)
+    ]
+    windows = []
+    for a in range(2):
+        for b in range(2):
+            near = jnp.where(col_low == b, own_n, beside_n)
+            away = jnp.where(col_low == b, above_n, corner_n)
+            windows.append(jnp.where(row_low == a, near, away).astype(BF16))
+    keys = dot(jnp.concatenate(windows, axis=0), wk_ref[...]).astype(BF16)
+    values_t = [dot_t(wv_t_ref[...], x).astype(BF16) for x in windows]
+    query_t = dot_t(wq_t_ref[...], own_n.astype(BF16)).astype(BF16)
 
     lanes = 256
     per = lanes // HD
-    head_of_lane = split(iota((1, lanes), 1), HD)[0]
-    window_parts = []
+    main = 128
+    rest = TOK - main
+    packed = per * TOK
+    lane = iota((1, packed), 1)
+    in_main = lane < per * main
+    token = jnp.where(in_main, split(lane, main)[1], main + split(lane, rest)[1])
+    _, token_row, token_col = token_coords(token)
+    label_row = (token_row >= WH - shift_row).astype(jnp.int32)
+    label = label_row * 2 + (token_col >= WW - shift_col).astype(jnp.int32)
+    outside = ((lat == 0) & (label_row == 0) & (row_low == 1)) | (
+        (lat == last_lat) & (label_row == 1) & (row_low == 0)
+    )
+    bias = jnp.where(outside, NEG_LARGE, 0.0)
+    head_of_row = split(iota((lanes, 1), 0), HD)[0]
+    rest_lane = iota((1, main), 1)
+    rest_head, rest_token = split(rest_lane, rest)
+    repeat = (iota((TOK, 1), 0) == main + rest_token).astype(F32).astype(BF16)
+    fold = (split(iota((main, 1), 0), rest)[1] == rest_lane).astype(F32).astype(BF16)
+    rest_mask = head_of_row == rest_head
+
+    def pick(parts, which):
+        return jnp.where(
+            which < 2,
+            jnp.where(which == 0, parts[0], parts[1]),
+            jnp.where(which == 2, parts[2], parts[3]),
+        )
+
+    main_parts = []
+    rest_parts = []
     for g in range(D // lanes):
-        query_g = query[:, g * lanes : (g + 1) * lanes]
-        key_g = keyval[:, g * lanes : (g + 1) * lanes]
-        value_g = keyval[:, D + g * lanes : D + (g + 1) * lanes]
-        total = jnp.zeros((TOK, lanes), F32)
+        lo = g * lanes
+        query_g = query_t[lo : lo + lanes]
+        query_main = query_g[:, :main].astype(F32)
+        blocks = [jnp.where(head_of_row == h, query_main, 0.0).astype(BF16) for h in range(per)]
+        blocks.append(jnp.where(rest_mask, dot(query_g, repeat), 0.0).astype(BF16))
+        scores_all = dot(keys[:, lo : lo + lanes], jnp.concatenate(blocks, axis=1))
+        scores = pick([scores_all[w * TOK : (w + 1) * TOK] for w in range(4)], label) + bias
+        powers = jnp.exp2((scores - jnp.max(scores, axis=0, keepdims=True)) * (SCALE * LOG2E))
+        weights = (powers * (1.0 / jnp.sum(powers, axis=0, keepdims=True))).astype(BF16)
         for h in range(per):
-            here = head_of_lane == h
-            scores = dot_t(query_g * here.astype(F32).astype(BF16), key_g) * SCALE + bias
-            powers = jnp.exp(scores - jnp.max(scores, axis=-1, keepdims=True))
-            weights = (powers * (1.0 / jnp.sum(powers, axis=-1, keepdims=True))).astype(BF16)
-            total = jnp.where(here, dot(weights, value_g), total)
-        window_parts.append(total.astype(BF16))
-    window_out = jnp.concatenate(window_parts, axis=1)
+            at = lo + h * HD
+            stacked = jnp.concatenate([v[at : at + HD] for v in values_t], axis=0)
+            result = dot(stacked, weights[:, h * main : (h + 1) * main])
+            main_parts.append(
+                pick([result[w * HD : (w + 1) * HD] for w in range(4)], label[:, :main])
+            )
+        stacked = jnp.concatenate([v[lo : lo + lanes] for v in values_t], axis=0)
+        result = dot(stacked, weights[:, per * main :])
+        picked = pick([result[w * lanes : (w + 1) * lanes] for w in range(4)], label[:, per * main :])
+        rest_parts.append(dot(jnp.where(rest_mask, picked, 0.0).astype(BF16), fold))
+    window_out = jnp.concatenate(
+        [
+            jnp.concatenate(main_parts, axis=0).T,
+            jnp.concatenate(rest_parts, axis=0).T[:rest],
+        ],
+        axis=0,
+    ).astype(BF16)
 
     middle = own + dot(window_out, wproj_ref[...])
-    mlp_in = layer_norm(middle, mlp_gain_ref[...].astype(F32)).astype(BF16)
+    mlp_in = layer_norm(middle, row_of(mlp_gain_ref)).astype(BF16)
     up = dot(mlp_in, wup_ref[...])
     inner = math.sqrt(2.0 / math.pi) * (up + 0.044715 * (up * up * up))
     hidden = (0.5 * up * (1.0 + jnp.tanh(inner))).astype(BF16)
     block_out = (middle + dot(hidden, wdown_ref[...])).astype(BF16)
 
-    groups = LATENT * WH // 2
-    rows = 8 * groups
+    count = (WH // 2) * (WW // 2) * LATENT
+    rows = (count + 7) // 8 * 8
     corner_index, place = split(iota((4 * rows, 1), 0), rows)
-    pair, col_pair = split(place, 8)
-    level, row_pair = split(pair, WH // 2)
+    pair, level = split(place, LATENT)
+    row_pair, col_pair = split(pair, WW // 2)
     corner_col, corner_row = split(corner_index, 2)
     source = level * (WH * WW) + (row_pair * 2 + corner_row) * WW + col_pair * 2 + corner_col
-    source = jnp.where(col_pair < WW // 2, source, -1)
+    source = jnp.where(place < count, source, -1)
     order = (iota((1, TOK), 1) == source).astype(F32).astype(BF16)
     sorted_out = dot(order, block_out)
     grouped = jnp.concatenate([sorted_out[i * rows : (i + 1) * rows] for i in range(4)], axis=1)
-    merge_in = layer_norm(grouped, merge_gain_ref[...].astype(F32)).astype(BF16)
+    merge_in = layer_norm(grouped, row_of(merge_gain_ref)).astype(BF16)
     merged = dot(merge_in, wmerge_ref[...])
-    for k in range(LATENT):
-        for i in range(WH // 2):
-            start = (k * (WH // 2) + i) * 8
-            out_ref[k, i] = merged[start : start + WW // 2].astype(BF16)
+    for i in range(WH // 2):
+        for j in range(WW // 2):
+            start = (i * (WW // 2) + j) * LATENT
+            out_ref[i, j] = merged[start : start + LATENT].astype(BF16)
 
 
 VMEM_SPEC = pl.BlockSpec(memory_space=pltpu.VMEM)
+HBM_SPEC = pl.BlockSpec(memory_space=pltpu.HBM)
 SMEM_SPEC = pl.BlockSpec(memory_space=pltpu.SMEM)
+
+
+def in_hbm(x):
+    return pltpu.with_memory_space_constraint(x, pltpu.HBM)
 
 
 def params(mib):
@@ -264,21 +344,32 @@
     cross_pairs = pairs(lats, lons, lambda a, o, v: (cross(a), o, 1 - v))
     corner_pairs = pairs(lats, lons, lambda a, o, v: (cross(a),) + aside(o, v))
 
-    enc_row = enc_gain.reshape(1, D)
     far_levels = lax.ppermute(levels_in, AXES, level_pairs)
     positions = levels_in.shape[0] * levels_in.shape[1] * levels_in.shape[2]
-    scores, values, query_rows = pl.pallas_call(
+    kept = (w_kv, w_cross_out, w_proj, w_up, w_down, w_merge)
+    scores, values, query_rows, wq_t, wv_t, wk, wkv, wcross, wproj, wup, wdown, wmerge = pl.pallas_call(
         local_kernel,
         out_shape=(
-            jax.ShapeDtypeStruct((positions, LATENT * HEADS), F32),
-            jax.ShapeDtypeStruct((positions, D), BF16),
-            jax.ShapeDtypeStruct((LATENT * HEADS, D), BF16),
-        ),
-        in_specs=[VMEM_SPEC] * 5,
-        out_specs=(VMEM_SPEC,) * 3,
-        compiler_params=params(24),
+            pltpu.VMEM((positions, LATENT * HEADS), F32),
+            pltpu.VMEM((positions, D), BF16),
+            pltpu.VMEM((LATENT * HEADS, D), BF16),
+        )
+        + (pltpu.VMEM((D, D), BF16),) * 3
+        + tuple(pltpu.VMEM(w.shape, BF16) for w in kept),
+        in_specs=[HBM_SPEC] + [VMEM_SPEC] * 2 + [HBM_SPEC] * 8,
+        out_specs=(VMEM_SPEC,) * 12,
+        scratch_shapes=[
+            pltpu.VMEM(levels_in.shape, BF16),
+            pltpu.VMEM(w_query.shape, BF16),
+            pltpu.VMEM(w_qkv.shape, BF16),
+            pltpu.SemaphoreType.DMA((9,)),
+        ],
+        compiler_params=params(14),
         name="local_levels",
-    )(levels_in, enc_row, latent_query, w_query, w_kv)
+    )(
+        in_hbm(levels_in), enc_gain, latent_query,
+        *[in_hbm(w) for w in (w_query, w_kv, w_qkv, w_cross_out, w_proj, w_up, w_down, w_merge)],
+    )
     both, own, other = pl.pallas_call(
         encode_kernel,
         out_shape=(
@@ -288,26 +379,26 @@
         ),
         in_specs=[VMEM_SPEC] * 8,
         out_specs=(VMEM_SPEC,) * 3,
-        compiler_params=params(24),
+        compiler_params=params(14),
         name="encode",
-    )(far_levels, scores, values, query_rows, enc_row, latent_query, w_kv, w_cross_out)
+    )(far_levels, scores, values, query_rows, enc_gain, latent_query, wkv, wcross)
     far = lax.ppermute(other, AXES, far_pairs)
     cross_far = lax.ppermute(own, AXES, corner_pairs)
     cross_both = lax.ppermute(both, AXES, cross_pairs)
     chip_both = lax.ppermute(both, AXES, chip_pairs)
     chip_far = lax.ppermute(far, AXES, chip_pairs)
-    return pl.pallas_call(
+    merged = pl.pallas_call(
         block_kernel,
-        out_shape=jax.ShapeDtypeStruct((LATENT, WH // 2, WW // 2, w_merge.shape[1]), BF16),
-        in_specs=[SMEM_SPEC] * 2 + [VMEM_SPEC] * 14,
+        out_shape=jax.ShapeDtypeStruct((WH // 2, WW // 2, LATENT, w_merge.shape[1]), BF16),
+        in_specs=[SMEM_SPEC] * 2 + [VMEM_SPEC] * 16,
         out_specs=VMEM_SPEC,
-        compiler_params=params(48),
+        compiler_params=params(24),
         name="window_block",
     )(
         shift_lat, shift_lon, both, far, chip_both, chip_far, cross_both, cross_far,
-        attn_gain.reshape(1, D), w_qkv, w_proj, mlp_gain.reshape(1, D), w_up, w_down,
-        merge_gain.reshape(1, 4 * D), w_merge,
-    )
+        attn_gain, wk, wq_t, wv_t, wproj, mlp_gain, wup, wdown, merge_gain, wmerge,
+    )
+    return merged.transpose(2, 0, 1, 3)
 
 
 def solution(mesh):

time: 51.5 us -> 42.2 us (0.82)
  local copies, waits for them, and re-layouts: 7.85 us -> 1.38 us
  Pallas kernels: 16 us -> 14.1 us
    unnamed x24 -> x10, local copies, waits for them, and re-layouts: 6.42 us -> 1.38 us
    pallas_call x2, Pallas kernels: 14.2 us -> 12.3 us  [the longest x1 7.46 us: on_device(): pl.pallas_call(block_kernel, out_shape=jax.ShapeDtypeStruct((WH // 2, WW...]
    ppermute x1, starting transfers between devices: 10.6 us -> 8.75 us  [on_device(): cross_both = lax.ppermute(both, AXES, cross_pairs)]
    ppermute x1, starting transfers between devices: 0.01 us -> 1.83 us  [on_device(): chip_both = lax.ppermute(both, AXES, chip_pairs)]
    reshape x4 -> x0, local copies, waits for them, and re-layouts: 0.73 us -> none  [the longest x1 0.71 us: on_device(): enc_row = enc_gain.reshape(1, D)]
    pallas_call x1 -> x0, local copies, waits for them, and re-layouts: 0.71 us -> none  [on_device(): pl.pallas_call(block_kernel, out_shape=jax.ShapeDtypeStruct((LATENT, WH /...]
  transfers between devices with their start and end apart: 6 -> 6, of which waited for: 2 -> 1; matrix products, arithmetic and copies ran while one was open for 1% -> 0% of each run, Pallas kernels for 2% -> 11%
where the time goes in v2:
time: 42.2 us; the launch traced here: 42.1 us
  starting transfers between devices  15.9 us (38%)
  Pallas kernels  14.1 us (33%)
  waiting for transfers between devices  9.26 us (22%)
  local copies, waits for them, and re-layouts  1.38 us (3%)
  between operations  1.38 us (3%)
    ppermute x1, waiting for transfers between devices, on_device(): cross_far = lax.ppermute(own, AXES, corner_pairs)  9.24 us
    ppermute x1, starting transfers between devices, on_device(): cross_both = lax.ppermute(both, AXES, cross_pairs)  8.75 us
    pallas_call x1, Pallas kernels, on_device(): pl.pallas_call(block_kernel, out_shape=jax.ShapeDtypeStruct((WH // 2, WW...  7.46 us
    pallas_call x1, Pallas kernels, on_device(): pl.pallas_call(local_kernel, out_shape=(pltpu.VMEM((positions, LATENT * H...  4.83 us
    ppermute x1, starting transfers between devices, on_device(): far = lax.ppermute(other, AXES, far_pairs)  2.25 us
    ppermute x1, starting transfers between devices, on_device(): far_levels = lax.ppermute(levels_in, AXES, level_pairs)  2.13 us
    pallas_call x1, Pallas kernels, on_device(): pl.pallas_call(encode_kernel, out_shape=(jax.ShapeDtypeStruct((2 * TOK, D...  1.83 us
    ppermute x1, starting transfers between devices, on_device(): chip_both = lax.ppermute(both, AXES, chip_pairs)  1.83 us
  transfers between devices with their start and end apart: 6, of which 1 were waited for; matrix products, arithmetic and copies ran while one was open for 0% of the time, Pallas kernels for 11%

profile of v2, /device:TPU:1, one launch (start us, length us, event | category | flops | bytes accessed | tf_op | source)
XLA Modules:
  0.0 42.1 jit_solution(1131148218245117659)
XLA Ops:
  0.0 2.1 %collective-permute-start = (bf16[2,6,24,512]{3,2,1,0:T(8,128)(2,1)}, bf16[2,6,24,512]{3,2,1,0:T(8,128)(2,1)S(1)}, u32[]{:S(2)}, u32[]{:S(2)}) collective-permute-start(bf16[2,6,24,512]{3,2,1,0:T(8,128)(2,1)} %levels_hbm.1), channel_id=1, source_target_pairs={{0,1},{1,0},{2,3},{3,2},{4,5},{5,4},{6,7},{7,6},{8,9},{9,8},{10,11... | collective-permute-start | bytes 884744 | tf_op jit(solution)/shard_map/ppermute | solution.py:347
  2.1 0.0 copy-start
  2.1 0.7 %copy-done = bf16[2,512]{1,0:T(2,128)(2,1)S(1)} copy-done((bf16[2,512]{1,0:T(2,128)(2,1)S(1)}, bf16[2,512]{1,0:T(2,128)(2,1)}, u32[]{:S(2)}) %copy-start) | copy-done | bytes 2072
  2.8 0.0 copy-start.1
  2.8 0.7 %copy-done.1 = bf16[512]{0:T(512)(128)(2,1)S(1)} copy-done((bf16[512]{0:T(512)(128)(2,1)S(1)}, bf16[512]{0:T(512)(128)(2,1)}, u32[]{:S(2)}) %copy-start.1) | copy-done | bytes 1048
  3.5 4.8 %local_levels.1 = (f32[288,32]{1,0:T(8,128)S(1)}, bf16[288,512]{1,0:T(8,128)(2,1)S(1)}, bf16[32,512]{1,0:T(8,128)(2,1)S(1)}, bf16[512,512]{1,0:T(8,128)(2,1)S(1)...) custom-call(bf16[2,6,24,512]{3,2,1,0:T(8,128)(2,1)} %levels_hbm.1, ...), custom_call_target="tpu_custom_call" | custom-call | tf_op jit(solution)/shard_map/local_levels/pallas_call | solution.py:350
  8.3 0.0 copy-start.2
  8.3 0.0 copy-start.3
  8.4 0.0 copy-start.4
  8.4 0.0 collective-permute-done.levels_ref
  8.4 1.8 %encode.1 = (bf16[288,512]{1,0:T(8,128)(2,1)S(1)}, bf16[144,512]{1,0:T(8,128)(2,1)S(1)}, bf16[144,512]{1,0:T(8,128)(2,1)S(1)}) custom-call(bf16[2,6,24,512]{3,2,1,0:T(8,128)(2,1)S(1)} %collective-permute-done.levels_ref, f32[288,32]{1,0:T(8,128)S(1)} %get-tuple-element.20.score_ref, bf16[288,512]{1,0:T(8,128)(2,1)S(1)} %get-tuple-element.21.value_ref, ...), custom_call_target="tpu_custom_call" | custom-call | tf_op jit(solution)/shard_map/encode/pallas_call | solution.py:373
  10.2 2.2 %collective-permute-start.1 = (bf16[144,512]{1,0:T(8,128)(2,1)S(1)}, bf16[144,512]{1,0:T(8,128)(2,1)S(1)}, u32[]{:S(2)}, u32[]{:S(2)}) collective-permute-start(bf16[144,512]{1,0:T(8,128)(2,1)S(1)} %get-tuple-element.26), channel_id=1, source_target_pairs={{0,2},{1,63},{2,4},{3,1},{4,6},{5,3},{6,8},{7,5},{8,10},{9,7},{10,... | collective-permute-start | bytes 442376 | tf_op jit(solution)/shard_map/ppermute | solution.py:385
  12.5 1.8 %collective-permute-start.2 = (bf16[288,512]{1,0:T(8,128)(2,1)S(1)}, bf16[288,512]{1,0:T(8,128)(2,1)S(1)}, u32[]{:S(2)}, u32[]{:S(2)}) collective-permute-start(bf16[288,512]{1,0:T(8,128)(2,1)S(1)} %get-tuple-element.25.both_ref), channel_id=1, source_target_pairs={{0,64},{1,65},{2,66},{3,67},{4,68},{5,69},{6,70},{7,71},{8,72},{9,... | collective-permute-start | bytes 884744 | tf_op jit(solution)/shard_map/ppermute | solution.py:388
  14.3 8.8 %collective-permute-start.4 = (bf16[288,512]{1,0:T(8,128)(2,1)S(1)}, bf16[288,512]{1,0:T(8,128)(2,1)S(1)}, u32[]{:S(2)}, u32[]{:S(2)}) collective-permute-start(bf16[288,512]{1,0:T(8,128)(2,1)S(1)} %get-tuple-element.25.both_ref), channel_id=1, source_target_pairs={{0,193},{1,192},{2,195},{3,194},{4,197},{5,196},{6,199},{7,198},{8... | collective-permute-start | bytes 884744 | tf_op jit(solution)/shard_map/ppermute | solution.py:387
  23.1 0.5 %collective-permute-start.5 = (bf16[144,512]{1,0:T(8,128)(2,1)S(1)}, bf16[144,512]{1,0:T(8,128)(2,1)S(1)}, u32[]{:S(2)}, u32[]{:S(2)}) collective-permute-start(bf16[144,512]{1,0:T(8,128)(2,1)S(1)} %get-tuple-element.27), channel_id=1, source_target_pairs={{0,255},{1,194},{2,193},{3,196},{4,195},{5,198},{6,197},{7,200},{8... | collective-permute-start | bytes 442376 | tf_op jit(solution)/shard_map/ppermute | solution.py:386
  23.5 0.0 collective-permute-done.1.far_ref
  23.5 0.5 %collective-permute-start.3 = (bf16[144,512]{1,0:T(8,128)(2,1)S(1)}, bf16[144,512]{1,0:T(8,128)(2,1)S(1)}, u32[]{:S(2)}, u32[]{:S(2)}) collective-permute-start(bf16[144,512]{1,0:T(8,128)(2,1)S(1)} %collective-permute-done.1.far_ref), channel_id=1, source_target_pairs={{0,64},{1,65},{2,66},{3,67},{4,68},{5,69},{6,70},{7,71},{8,72},{9,... | collective-permute-start | bytes 442376 | tf_op jit(solution)/shard_map/ppermute | solution.py:389
  25.3 9.2 %collective-permute-done.5.cross_far_ref = bf16[144,512]{1,0:T(8,128)(2,1)S(1)} collective-permute-done((bf16[144,512]{1,0:T(8,128)(2,1)S(1)}, bf16[144,512]{1,0:T(8,128)(2,1)S(1)}, u32[]{:S(2)}, u32[]{:S(2)}) %collective-permute-start.5) | collective-permute-done | bytes 147488 | tf_op jit(solution)/shard_map/ppermute | solution.py:386
  34.6 0.0 collective-permute-done.3.chip_far_ref
  34.6 0.0 collective-permute-done.2.chip_ref
  34.6 0.0 collective-permute-done.4.cross_ref
  34.6 0.0 copy-done.2
  34.6 0.0 copy-done.3
  34.6 0.0 copy-done.4
  34.6 7.5 %window_block.1 = bf16[3,6,2,1024]{3,2,1,0:T(2,128)(2,1)} custom-call(s32[1]{0:T(128)S(6)} %copy.17.shift_lat_ref, s32[1]{0:T(128)S(6)} %copy.18.shift_lon_ref, bf16[288,512]{1,0:T(8,128)(2,1)S(1)} %get-tuple-element.25.both_ref, bf16[144,512]{1,0:T(8,128)(2,1)S(1)} %collective-permute-done.1.far_ref, bf16[288,512]{1,0:T(8,128)(2,1)S(1)} %collective-permute-done.2.chip_ref, ...), custom_call_target="tpu_custom_call" | custom-call | tf_op jit(solution)/shard_map/window_block/pallas_call | solution.py:390
Async XLA Ops:
  0.0 8.4 %collective-permute-start = (bf16[2,6,24,512]{3,2,1,0:T(8,128)(2,1)}, bf16[2,6,24,512]{3,2,1,0:T(8,128)(2,1)S(1)}, u32[]{:S(2)}, u32[]{:S(2)}) collective-permute-start(bf16[2,6,24,512]{3,2,1,0:T(8,128)(2,1)} %levels_hbm.1), channel_id=1, source_target_pairs={{0,1},{1,0},{2,3},{3,2},{4,5},{5,4},{6,7},{7,6},{8,9},{9,8},{10,11... | collective-permute-start | bytes 884744 | tf_op jit(solution)/shard_map/ppermute | solution.py:347
  2.1 0.7 %copy-start = (bf16[2,512]{1,0:T(2,128)(2,1)S(1)}, bf16[2,512]{1,0:T(2,128)(2,1)}, u32[]{:S(2)}) copy-start(bf16[2,512]{1,0:T(2,128)(2,1)} %lq_ref.3) | copy-start | bytes 6148
  2.8 0.7 %copy-start.1 = (bf16[512]{0:T(512)(128)(2,1)S(1)}, bf16[512]{0:T(512)(128)(2,1)}, u32[]{:S(2)}) copy-start(bf16[512]{0:T(512)(128)(2,1)} %gain_ref.3) | copy-start | bytes 3076
  8.3 26.2 %copy-start.2 = (bf16[2048]{0:T(1024)(128)(2,1)S(1)}, bf16[2048]{0:T(1024)(128)(2,1)}, u32[]{:S(2)}) copy-start(bf16[2048]{0:T(1024)(128)(2,1)} %merge_gain_ref.1) | copy-start | bytes 12292
  8.3 26.2 %copy-start.3 = (bf16[512]{0:T(512)(128)(2,1)S(1)}, bf16[512]{0:T(512)(128)(2,1)}, u32[]{:S(2)}) copy-start(bf16[512]{0:T(512)(128)(2,1)} %attn_gain_ref.1) | copy-start | bytes 3076
  8.4 26.2 %copy-start.4 = (bf16[512]{0:T(512)(128)(2,1)S(1)}, bf16[512]{0:T(512)(128)(2,1)}, u32[]{:S(2)}) copy-start(bf16[512]{0:T(512)(128)(2,1)} %mlp_gain_ref.1) | copy-start | bytes 3076
  10.2 13.3 %collective-permute-start.1 = (bf16[144,512]{1,0:T(8,128)(2,1)S(1)}, bf16[144,512]{1,0:T(8,128)(2,1)S(1)}, u32[]{:S(2)}, u32[]{:S(2)}) collective-permute-start(bf16[144,512]{1,0:T(8,128)(2,1)S(1)} %get-tuple-element.26), channel_id=1, source_target_pairs={{0,2},{1,63},{2,4},{3,1},{4,6},{5,3},{6,8},{7,5},{8,10},{9,7},{10,... | collective-permute-start | bytes 442376 | tf_op jit(solution)/shard_map/ppermute | solution.py:385
  12.5 22.1 %collective-permute-start.2 = (bf16[288,512]{1,0:T(8,128)(2,1)S(1)}, bf16[288,512]{1,0:T(8,128)(2,1)S(1)}, u32[]{:S(2)}, u32[]{:S(2)}) collective-permute-start(bf16[288,512]{1,0:T(8,128)(2,1)S(1)} %get-tuple-element.25.both_ref), channel_id=1, source_target_pairs={{0,64},{1,65},{2,66},{3,67},{4,68},{5,69},{6,70},{7,71},{8,72},{9,... | collective-permute-start | bytes 884744 | tf_op jit(solution)/shard_map/ppermute | solution.py:388
  14.3 20.3 %collective-permute-start.4 = (bf16[288,512]{1,0:T(8,128)(2,1)S(1)}, bf16[288,512]{1,0:T(8,128)(2,1)S(1)}, u32[]{:S(2)}, u32[]{:S(2)}) collective-permute-start(bf16[288,512]{1,0:T(8,128)(2,1)S(1)} %get-tuple-element.25.both_ref), channel_id=1, source_target_pairs={{0,193},{1,192},{2,195},{3,194},{4,197},{5,196},{6,199},{7,198},{8... | collective-permute-start | bytes 884744 | tf_op jit(solution)/shard_map/ppermute | solution.py:387
  23.1 11.5 %collective-permute-start.5 = (bf16[144,512]{1,0:T(8,128)(2,1)S(1)}, bf16[144,512]{1,0:T(8,128)(2,1)S(1)}, u32[]{:S(2)}, u32[]{:S(2)}) collective-permute-start(bf16[144,512]{1,0:T(8,128)(2,1)S(1)} %get-tuple-element.27), channel_id=1, source_target_pairs={{0,255},{1,194},{2,193},{3,196},{4,195},{5,198},{6,197},{7,200},{8... | collective-permute-start | bytes 442376 | tf_op jit(solution)/shard_map/ppermute | solution.py:386
  23.5 11.1 %collective-permute-start.3 = (bf16[144,512]{1,0:T(8,128)(2,1)S(1)}, bf16[144,512]{1,0:T(8,128)(2,1)S(1)}, u32[]{:S(2)}, u32[]{:S(2)}) collective-permute-start(bf16[144,512]{1,0:T(8,128)(2,1)S(1)} %collective-permute-done.1.far_ref), channel_id=1, source_target_pairs={{0,64},{1,65},{2,66},{3,67},{4,68},{5,69},{6,70},{7,71},{8,72},{9,... | collective-permute-start | bytes 442376 | tf_op jit(solution)/shard_map/ppermute | solution.py:389

commit v3 on v2

--- a/solution.py
+++ b/solution.py
@@ -115,7 +115,7 @@
 
 def encode_kernel(
     levels_ref, score_ref, value_ref, query_ref, gain_ref, lq_ref, wkv_ref, wcross_ref,
-    both_ref, own_ref, other_ref,
+    both_ref,
 ):
     lev = lax.axis_index("lev")
     keyval = level_keyval(levels_ref, row_of(gain_ref), wkv_ref[...])
@@ -151,8 +151,11 @@
     order = (iota((1, 2 * TOK), 1) == source).astype(F32).astype(BF16)
     both = dot(order, latents).astype(BF16)
     both_ref[...] = both
-    own_ref[...] = both[:TOK]
-    other_ref[...] = both[TOK:]
+
+
+def halves_kernel(both_ref, chip_ref, own_ref, other_ref):
+    own_ref[...] = both_ref[:TOK]
+    other_ref[...] = both_ref[TOK:]
 
 
 def block_kernel(
@@ -341,8 +344,15 @@
     level_pairs = pairs(lats, lons, lambda a, o, v: (a, o, 1 - v))
     far_pairs = pairs(lats, lons, lambda a, o, v: (a, o + 1 if v == 0 else o - 1, v))
     chip_pairs = pairs(lats, lons, lambda a, o, v: (chip(a), o, v))
-    cross_pairs = pairs(lats, lons, lambda a, o, v: (cross(a), o, 1 - v))
-    corner_pairs = pairs(lats, lons, lambda a, o, v: (cross(a),) + aside(o, v))
+    def edge(a):
+        return a == 0 or a == lats - 1
+
+    cross_pairs = pairs(
+        lats, lons, lambda a, o, v: (a if edge(a) else cross(a), o, 1 - v)
+    )
+    corner_pairs = pairs(
+        lats, lons, lambda a, o, v: (a, o, 1 - v) if edge(a) else (cross(a),) + aside(o, v)
+    )
 
     far_levels = lax.ppermute(levels_in, AXES, level_pairs)
     positions = levels_in.shape[0] * levels_in.shape[1] * levels_in.shape[2]
@@ -370,22 +380,26 @@
         in_hbm(levels_in), enc_gain, latent_query,
         *[in_hbm(w) for w in (w_query, w_kv, w_qkv, w_cross_out, w_proj, w_up, w_down, w_merge)],
     )
-    both, own, other = pl.pallas_call(
+    both = pl.pallas_call(
         encode_kernel,
-        out_shape=(
-            jax.ShapeDtypeStruct((2 * TOK, D), BF16),
-            jax.ShapeDtypeStruct((TOK, D), BF16),
-            jax.ShapeDtypeStruct((TOK, D), BF16),
-        ),
+        out_shape=jax.ShapeDtypeStruct((2 * TOK, D), BF16),
         in_specs=[VMEM_SPEC] * 8,
-        out_specs=(VMEM_SPEC,) * 3,
+        out_specs=VMEM_SPEC,
         compiler_params=params(14),
         name="encode",
     )(far_levels, scores, values, query_rows, enc_gain, latent_query, wkv, wcross)
+    chip_both = lax.ppermute(both, AXES, chip_pairs)
+    cross_both = lax.ppermute(both, AXES, cross_pairs)
+    own, other = pl.pallas_call(
+        halves_kernel,
+        out_shape=(jax.ShapeDtypeStruct((TOK, D), BF16),) * 2,
+        in_specs=[VMEM_SPEC, pl.BlockSpec(memory_space=pl.ANY)],
+        out_specs=(VMEM_SPEC,) * 2,
+        compiler_params=params(2),
+        name="halves",
+    )(both, chip_both)
     far = lax.ppermute(other, AXES, far_pairs)
     cross_far = lax.ppermute(own, AXES, corner_pairs)
-    cross_both = lax.ppermute(both, AXES, cross_pairs)
-    chip_both = lax.ppermute(both, AXES, chip_pairs)
     chip_far = lax.ppermute(far, AXES, chip_pairs)
     merged = pl.pallas_call(
         block_kernel,

time: 42.2 us -> 35.6 us (0.84)
  waiting for transfers between devices: 9.26 us -> 1.52 us
  starting transfers between devices: 15.9 us -> 17.1 us
    ppermute x1, waiting for transfers between devices: 9.24 us -> 0.46 us  [on_device(): cross_far = lax.ppermute(own, AXES, corner_pairs)]
    ppermute x1, starting transfers between devices: 0.45 us -> 8.33 us  [on_device(): cross_far = lax.ppermute(own, AXES, corner_pairs)]
    ppermute x1, starting transfers between devices: 8.75 us -> 2.88 us  [on_device(): cross_both = lax.ppermute(both, AXES, cross_pairs)]
    ppermute x1, waiting for transfers between devices: 0.01 us -> 1.05 us  [on_device(): far = lax.ppermute(other, AXES, far_pairs)]
    ppermute x1, starting transfers between devices: 2.25 us -> 1.72 us  [on_device(): far = lax.ppermute(other, AXES, far_pairs)]
    ppermute x1, starting transfers between devices: 0.51 us -> 0.01 us  [on_device(): chip_far = lax.ppermute(far, AXES, chip_pairs)]
    pallas_call x1 -> x2, Pallas kernels: 1.83 us -> 1.85 us  [the longest x1 1.83 us: on_device(): pl.pallas_call(encode_kernel, out_shape=jax.ShapeDtypeStruct((2 * TOK, D)...]
  transfers between devices with their start and end apart: 6 -> 6, of which waited for: 1 -> 2; matrix products, arithmetic and copies ran while one was open for 0% -> 0% of each run, Pallas kernels for 11% -> 14%
where the time goes in v3:
time: 35.6 us; the launch traced here: 35.5 us
  starting transfers between devices  17.1 us (48%)
  Pallas kernels  14.1 us (40%)
  waiting for transfers between devices  1.52 us (4%)
  local copies, waits for them, and re-layouts  1.38 us (4%)
  between operations  1.38 us (4%)
    ppermute x1, starting transfers between devices, on_device(): cross_far = lax.ppermute(own, AXES, corner_pairs)  8.33 us
    pallas_call x1, Pallas kernels, on_device(): pl.pallas_call(block_kernel, out_shape=jax.ShapeDtypeStruct((WH // 2, WW...  7.47 us
    pallas_call x1, Pallas kernels, on_device(): pl.pallas_call(local_kernel, out_shape=(pltpu.VMEM((positions, LATENT * H...  4.83 us
    ppermute x1, starting transfers between devices, on_device(): cross_both = lax.ppermute(both, AXES, cross_pairs)  2.88 us
    ppermute x1, starting transfers between devices, on_device(): far_levels = lax.ppermute(levels_in, AXES, level_pairs)  2.13 us
    ppermute x1, starting transfers between devices, on_device(): chip_both = lax.ppermute(both, AXES, chip_pairs)  2.01 us
    pallas_call x1, Pallas kernels, on_device(): pl.pallas_call(encode_kernel, out_shape=jax.ShapeDtypeStruct((2 * TOK, D)...  1.83 us
    ppermute x1, starting transfers between devices, on_device(): far = lax.ppermute(other, AXES, far_pairs)  1.72 us
  transfers between devices with their start and end apart: 6, of which 2 were waited for; matrix products, arithmetic and copies ran while one was open for 0% of the time, Pallas kernels for 14%

profile of v3, /device:TPU:1, one launch (start us, length us, event | category | flops | bytes accessed | tf_op | source)
XLA Modules:
  0.0 35.5 jit_solution(6887509832900969748)
XLA Ops:
  0.0 2.1 %collective-permute-start = (bf16[2,6,24,512]{3,2,1,0:T(8,128)(2,1)}, bf16[2,6,24,512]{3,2,1,0:T(8,128)(2,1)S(1)}, u32[]{:S(2)}, u32[]{:S(2)}) collective-permute-start(bf16[2,6,24,512]{3,2,1,0:T(8,128)(2,1)} %levels_hbm.1), channel_id=1, source_target_pairs={{0,1},{1,0},{2,3},{3,2},{4,5},{5,4},{6,7},{7,6},{8,9},{9,8},{10,11... | collective-permute-start | bytes 884744 | tf_op jit(solution)/shard_map/ppermute | solution.py:357
  2.1 0.0 copy-start
  2.1 0.7 %copy-done = bf16[2,512]{1,0:T(2,128)(2,1)S(1)} copy-done((bf16[2,512]{1,0:T(2,128)(2,1)S(1)}, bf16[2,512]{1,0:T(2,128)(2,1)}, u32[]{:S(2)}) %copy-start) | copy-done | bytes 2072
  2.8 0.0 copy-start.2
  2.8 0.7 %copy-done.2 = bf16[512]{0:T(512)(128)(2,1)S(1)} copy-done((bf16[512]{0:T(512)(128)(2,1)S(1)}, bf16[512]{0:T(512)(128)(2,1)}, u32[]{:S(2)}) %copy-start.2) | copy-done | bytes 1048
  3.5 4.8 %local_levels.1 = (f32[288,32]{1,0:T(8,128)S(1)}, bf16[288,512]{1,0:T(8,128)(2,1)S(1)}, bf16[32,512]{1,0:T(8,128)(2,1)S(1)}, bf16[512,512]{1,0:T(8,128)(2,1)S(1)...) custom-call(bf16[2,6,24,512]{3,2,1,0:T(8,128)(2,1)} %levels_hbm.1, ...), custom_call_target="tpu_custom_call" | custom-call | tf_op jit(solution)/shard_map/local_levels/pallas_call | solution.py:360
  8.3 0.0 copy-start.1
  8.3 0.0 copy-start.3
  8.4 0.0 copy-start.4
  8.4 0.0 collective-permute-done.levels_ref
  8.4 1.8 %encode.1.both_ref = bf16[288,512]{1,0:T(8,128)(2,1)S(1)} custom-call(bf16[2,6,24,512]{3,2,1,0:T(8,128)(2,1)S(1)} %collective-permute-done.levels_ref, f32[288,32]{1,0:T(8,128)S(1)} %get-tuple-element.19.score_ref, bf16[288,512]{1,0:T(8,128)(2,1)S(1)} %get-tuple-element.20.value_ref, bf16[32,512]{1,0:T(8,128)(2,1)S(1)} %get-tuple-element.21.query_ref, ...), custom_call_target="tpu_custom_call" | custom-call | tf_op jit(solution)/shard_map/encode/pallas_call | solution.py:383
  10.2 2.0 %collective-permute-start.1 = (bf16[288,512]{1,0:T(8,128)(2,1)S(1)}, bf16[288,512]{1,0:T(8,128)(2,1)S(1)}, u32[]{:S(2)}, u32[]{:S(2)}) collective-permute-start(bf16[288,512]{1,0:T(8,128)(2,1)S(1)} %encode.1.both_ref), channel_id=1, source_target_pairs={{0,64},{1,65},{2,66},{3,67},{4,68},{5,69},{6,70},{7,71},{8,72},{9,... | collective-permute-start | bytes 884744 | tf_op jit(solution)/shard_map/ppermute | solution.py:391
  12.2 2.9 %collective-permute-start.4 = (bf16[288,512]{1,0:T(8,128)(2,1)S(1)}, bf16[288,512]{1,0:T(8,128)(2,1)S(1)}, u32[]{:S(2)}, u32[]{:S(2)}) collective-permute-start(bf16[288,512]{1,0:T(8,128)(2,1)S(1)} %encode.1.both_ref), channel_id=1, source_target_pairs={{0,1},{1,0},{2,3},{3,2},{4,5},{5,4},{6,7},{7,6},{8,9},{9,8},{10,11... | collective-permute-start | bytes 884744 | tf_op jit(solution)/shard_map/ppermute | solution.py:392
  15.1 0.0 collective-permute-done.1.chip_ref
  15.1 1.7 %collective-permute-start.2 = (bf16[144,512]{1,0:T(8,128)(2,1)S(1)}, bf16[144,512]{1,0:T(8,128)(2,1)S(1)}, u32[]{:S(2)}, u32[]{:S(2)}) collective-permute-start(bf16[144,512]{1,0:T(8,128)(2,1)S(1)} %get-tuple-element.24), channel_id=1, source_target_pairs={{0,2},{1,63},{2,4},{3,1},{4,6},{5,3},{6,8},{7,5},{8,10},{9,7},{10,... | collective-permute-start | bytes 442376 | tf_op jit(solution)/shard_map/ppermute | solution.py:401
  16.9 8.3 %collective-permute-start.5 = (bf16[144,512]{1,0:T(8,128)(2,1)S(1)}, bf16[144,512]{1,0:T(8,128)(2,1)S(1)}, u32[]{:S(2)}, u32[]{:S(2)}) collective-permute-start(bf16[144,512]{1,0:T(8,128)(2,1)S(1)} %get-tuple-element.25), channel_id=1, source_target_pairs={{0,1},{1,0},{2,3},{3,2},{4,5},{5,4},{6,7},{7,6},{8,9},{9,8},{10,11... | collective-permute-start | bytes 442376 | tf_op jit(solution)/shard_map/ppermute | solution.py:402
  25.2 1.0 %collective-permute-done.2.far_ref = bf16[144,512]{1,0:T(8,128)(2,1)S(1)} collective-permute-done((bf16[144,512]{1,0:T(8,128)(2,1)S(1)}, bf16[144,512]{1,0:T(8,128)(2,1)S(1)}, u32[]{:S(2)}, u32[]{:S(2)}) %collective-permute-start.2) | collective-permute-done | bytes 147488 | tf_op jit(solution)/shard_map/ppermute | solution.py:401
  26.2 0.0 collective-permute-start.3
  27.5 0.0 collective-permute-done.4.cross_ref
  27.5 0.5 %collective-permute-done.5.cross_far_ref = bf16[144,512]{1,0:T(8,128)(2,1)S(1)} collective-permute-done((bf16[144,512]{1,0:T(8,128)(2,1)S(1)}, bf16[144,512]{1,0:T(8,128)(2,1)S(1)}, u32[]{:S(2)}, u32[]{:S(2)}) %collective-permute-start.5) | collective-permute-done | bytes 147488 | tf_op jit(solution)/shard_map/ppermute | solution.py:402
  28.0 0.0 collective-permute-done.3.chip_far_ref
  28.0 0.0 copy-done.1
  28.0 0.0 copy-done.3
  28.0 0.0 copy-done.4
  28.0 7.5 %window_block.1 = bf16[3,6,2,1024]{3,2,1,0:T(2,128)(2,1)} custom-call(s32[1]{0:T(128)S(6)} %copy.17.shift_lat_ref, s32[1]{0:T(128)S(6)} %copy.18.shift_lon_ref, bf16[288,512]{1,0:T(8,128)(2,1)S(1)} %encode.1.both_ref, bf16[144,512]{1,0:T(8,128)(2,1)S(1)} %collective-permute-done.2.far_ref, bf16[288,512]{1,0:T(8,128)(2,1)S(1)} %collective-permute-done.1.chip_ref, ...), custom_call_target="tpu_custom_call" | custom-call | tf_op jit(solution)/shard_map/window_block/pallas_call | solution.py:404
  (1 shorter events, 0.0 us)
Async XLA Ops:
  0.0 8.4 %collective-permute-start = (bf16[2,6,24,512]{3,2,1,0:T(8,128)(2,1)}, bf16[2,6,24,512]{3,2,1,0:T(8,128)(2,1)S(1)}, u32[]{:S(2)}, u32[]{:S(2)}) collective-permute-start(bf16[2,6,24,512]{3,2,1,0:T(8,128)(2,1)} %levels_hbm.1), channel_id=1, source_target_pairs={{0,1},{1,0},{2,3},{3,2},{4,5},{5,4},{6,7},{7,6},{8,9},{9,8},{10,11... | collective-permute-start | bytes 884744 | tf_op jit(solution)/shard_map/ppermute | solution.py:357
  2.1 0.7 %copy-start = (bf16[2,512]{1,0:T(2,128)(2,1)S(1)}, bf16[2,512]{1,0:T(2,128)(2,1)}, u32[]{:S(2)}) copy-start(bf16[2,512]{1,0:T(2,128)(2,1)} %lq_ref.3) | copy-start | bytes 6148
  2.8 0.7 %copy-start.2 = (bf16[512]{0:T(512)(128)(2,1)S(1)}, bf16[512]{0:T(512)(128)(2,1)}, u32[]{:S(2)}) copy-start(bf16[512]{0:T(512)(128)(2,1)} %gain_ref.3) | copy-start | bytes 3076
  8.3 19.7 %copy-start.1 = (bf16[2048]{0:T(1024)(128)(2,1)S(1)}, bf16[2048]{0:T(1024)(128)(2,1)}, u32[]{:S(2)}) copy-start(bf16[2048]{0:T(1024)(128)(2,1)} %merge_gain_ref.1) | copy-start | bytes 12292
  8.3 19.7 %copy-start.3 = (bf16[512]{0:T(512)(128)(2,1)S(1)}, bf16[512]{0:T(512)(128)(2,1)}, u32[]{:S(2)}) copy-start(bf16[512]{0:T(512)(128)(2,1)} %attn_gain_ref.1) | copy-start | bytes 3076
  8.4 19.7 %copy-start.4 = (bf16[512]{0:T(512)(128)(2,1)S(1)}, bf16[512]{0:T(512)(128)(2,1)}, u32[]{:S(2)}) copy-start(bf16[512]{0:T(512)(128)(2,1)} %mlp_gain_ref.1) | copy-start | bytes 3076
  10.2 4.9 %collective-permute-start.1 = (bf16[288,512]{1,0:T(8,128)(2,1)S(1)}, bf16[288,512]{1,0:T(8,128)(2,1)S(1)}, u32[]{:S(2)}, u32[]{:S(2)}) collective-permute-start(bf16[288,512]{1,0:T(8,128)(2,1)S(1)} %encode.1.both_ref), channel_id=1, source_target_pairs={{0,64},{1,65},{2,66},{3,67},{4,68},{5,69},{6,70},{7,71},{8,72},{9,... | collective-permute-start | bytes 884744 | tf_op jit(solution)/shard_map/ppermute | solution.py:391
  12.2 15.3 %collective-permute-start.4 = (bf16[288,512]{1,0:T(8,128)(2,1)S(1)}, bf16[288,512]{1,0:T(8,128)(2,1)S(1)}, u32[]{:S(2)}, u32[]{:S(2)}) collective-permute-start(bf16[288,512]{1,0:T(8,128)(2,1)S(1)} %encode.1.both_ref), channel_id=1, source_target_pairs={{0,1},{1,0},{2,3},{3,2},{4,5},{5,4},{6,7},{7,6},{8,9},{9,8},{10,11... | collective-permute-start | bytes 884744 | tf_op jit(solution)/shard_map/ppermute | solution.py:392
  15.1 11.1 %collective-permute-start.2 = (bf16[144,512]{1,0:T(8,128)(2,1)S(1)}, bf16[144,512]{1,0:T(8,128)(2,1)S(1)}, u32[]{:S(2)}, u32[]{:S(2)}) collective-permute-start(bf16[144,512]{1,0:T(8,128)(2,1)S(1)} %get-tuple-element.24), channel_id=1, source_target_pairs={{0,2},{1,63},{2,4},{3,1},{4,6},{5,3},{6,8},{7,5},{8,10},{9,7},{10,... | collective-permute-start | bytes 442376 | tf_op jit(solution)/shard_map/ppermute | solution.py:401
  16.9 11.2 %collective-permute-start.5 = (bf16[144,512]{1,0:T(8,128)(2,1)S(1)}, bf16[144,512]{1,0:T(8,128)(2,1)S(1)}, u32[]{:S(2)}, u32[]{:S(2)}) collective-permute-start(bf16[144,512]{1,0:T(8,128)(2,1)S(1)} %get-tuple-element.25), channel_id=1, source_target_pairs={{0,1},{1,0},{2,3},{3,2},{4,5},{5,4},{6,7},{7,6},{8,9},{9,8},{10,11... | collective-permute-start | bytes 442376 | tf_op jit(solution)/shard_map/ppermute | solution.py:402
  26.2 1.8 %collective-permute-start.3 = (bf16[144,512]{1,0:T(8,128)(2,1)S(1)}, bf16[144,512]{1,0:T(8,128)(2,1)S(1)}, u32[]{:S(2)}, u32[]{:S(2)}) collective-permute-start(bf16[144,512]{1,0:T(8,128)(2,1)S(1)} %collective-permute-done.2.far_ref), channel_id=1, source_target_pairs={{0,64},{1,65},{2,66},{3,67},{4,68},{5,69},{6,70},{7,71},{8,72},{9,... | collective-permute-start | bytes 442376 | tf_op jit(solution)/shard_map/ppermute | solution.py:403

commit v4 on v3

--- a/solution.py
+++ b/solution.py
@@ -67,11 +67,11 @@
 
 
 def local_kernel(
-    levels_hbm, gain_ref, lq_ref, wq_hbm, wkv_hbm, wqkv_hbm, wcross_hbm, wproj_hbm, wup_hbm,
+    shift_lat_ref, shift_lon_ref, levels_hbm, gain_hbm, lq_hbm, wq_hbm, wkv_hbm, wqkv_hbm, wcross_hbm, wproj_hbm, wup_hbm,
     wdown_hbm, wmerge_hbm,
     score_ref, value_ref, query_ref, wq_t_ref, wv_t_ref, wk_ref, wkv_ref, wcross_ref, wproj_ref,
-    wup_ref, wdown_ref, wmerge_ref,
-    levels_ref, wq_ref, wqkv_ref, sems,
+    wup_ref, wdown_ref, wmerge_ref, shift_ref,
+    gain_ref, lq_ref, levels_ref, wq_ref, wqkv_ref, sems,
 ):
     moves = [
         (levels_hbm, levels_ref),
@@ -83,15 +83,18 @@
         (wup_hbm, wup_ref),
         (wdown_hbm, wdown_ref),
         (wmerge_hbm, wmerge_ref),
+        (gain_hbm, gain_ref),
+        (lq_hbm, lq_ref),
     ]
     copies = [
         pltpu.make_async_copy(source, target, sems.at[i])
         for i, (source, target) in enumerate(moves)
     ]
-    for copy in copies:
+    for copy in copies[9:] + copies[:9]:
         copy.start()
-    copies[0].wait()
-    copies[1].wait()
+    shift_ref[...] = jnp.where(iota((8, 128), 0) == 0, shift_lat_ref[0], shift_lon_ref[0])
+    for copy in copies[9:] + copies[:2]:
+        copy.wait()
     keyval = level_keyval(levels_ref, row_of(gain_ref), wkv_ref[...])
     value_ref[...] = keyval[:, D:]
     copies[2].wait()
@@ -109,7 +112,7 @@
     wq_t_ref[...] = wqkv_ref[:, :D].astype(F32).T.astype(BF16)
     wk_ref[...] = wqkv_ref[:, D : 2 * D]
     wv_t_ref[...] = wqkv_ref[:, 2 * D :].astype(F32).T.astype(BF16)
-    for copy in copies[4:]:
+    for copy in copies[4:9]:
         copy.wait()
 
 
@@ -158,70 +161,128 @@
     other_ref[...] = both_ref[TOK:]
 
 
+LANES = 256
+PER = LANES // HD
+MAIN = 128
+REST = TOK - MAIN
+PACKED = PER * TOK
+GROUPS = D // LANES
+
+
+def shifted(row, col, shift_ref):
+    low_row = (row >= WH - shift_ref[0:1, 0:1]).astype(jnp.int32)
+    low_col = (col >= WW - shift_ref[1:2, 0:1]).astype(jnp.int32)
+    return low_row, low_col
+
+
+def key_places(shift_ref):
+    _, row, col = token_coords(iota((TOK, 1), 0))
+    return shifted(row, col, shift_ref)
+
+
+def query_places(shift_ref):
+    lane = iota((1, PACKED), 1)
+    token = jnp.where(
+        lane < PER * MAIN, split(lane, MAIN)[1], MAIN + split(lane, REST)[1]
+    )
+    _, row, col = token_coords(token)
+    return shifted(row, col, shift_ref)
+
+
+def rest_places():
+    lane = iota((1, MAIN), 1)
+    head, token = split(lane, REST)
+    return head, token, split(iota((LANES, 1), 0), HD)[0] == head
+
+
+def near_kernel(
+    shift_ref, both_ref, far_ref, chip_ref, cross_ref, gain_ref, wk_ref, wq_t_ref, wv_t_ref,
+    score_ref, mark_ref, query_ref, value_ref,
+):
+    lat = lax.axis_index("lat")
+    lev = lax.axis_index("lev")
+    last_lat = lax.axis_size("lat") - 1
+    row_low, col_low = key_places(shift_ref)
+    own = both_ref[:TOK].astype(F32)
+    beside = jnp.where(col_low == lev, both_ref[TOK:].astype(F32), far_ref[...].astype(F32))
+    above = jnp.where(
+        row_low == lat % 2, chip_ref[:TOK].astype(F32), cross_ref[TOK:].astype(F32)
+    )
+    tokens = jnp.concatenate([own, beside, above], axis=0)
+    normed = layer_norm(tokens, row_of(gain_ref)).astype(BF16)
+    keys = dot(normed, wk_ref[...]).astype(BF16)
+    query_t = dot_t(wq_t_ref[...], normed[:TOK]).astype(BF16)
+
+    label_row, label_col = query_places(shift_ref)
+    same_row = label_row == row_low
+    same_col = label_col == col_low
+    outside = (~same_row) & (
+        ((lat == 0) & (row_low == 1)) | ((lat == last_lat) & (row_low == 0))
+    )
+    bias = jnp.where(outside, NEG_LARGE, 0.0)
+    mark_ref[...] = jnp.where(same_row | same_col, 1.0, bias)
+    _, rest_token, rest_mask = rest_places()
+    head_of_row = split(iota((LANES, 1), 0), HD)[0]
+    repeat = (iota((TOK, 1), 0) == MAIN + rest_token).astype(F32).astype(BF16)
+    for g in range(GROUPS):
+        lo = g * LANES
+        query_g = query_t[lo : lo + LANES]
+        query_main = query_g[:, :MAIN].astype(F32)
+        blocks = [jnp.where(head_of_row == h, query_main, 0.0).astype(BF16) for h in range(PER)]
+        blocks.append(jnp.where(rest_mask, dot(query_g, repeat), 0.0).astype(BF16))
+        packed = jnp.concatenate(blocks, axis=1)
+        query_ref[lo : lo + LANES] = packed
+        scores = dot(keys[:, lo : lo + LANES], packed)
+        score_ref[g] = bias + jnp.where(
+            same_row,
+            jnp.where(same_col, scores[:TOK], scores[TOK : 2 * TOK]),
+            scores[2 * TOK :],
+        )
+
+    _, lane_row, lane_col = token_coords(iota((1, TOK), 1))
+    lane_row, lane_col = shifted(lane_row, lane_col, shift_ref)
+    values = [
+        dot_t(wv_t_ref[...], normed[i * TOK : (i + 1) * TOK]) for i in range(3)
+    ]
+    for w in range(4):
+        in_row = lane_row == w // 2
+        in_col = lane_col == w % 2
+        window = jnp.where(
+            in_row,
+            jnp.where(in_col, values[0], values[1]),
+            jnp.where(in_col, values[2], 0.0),
+        ).astype(BF16)
+        for h in range(HEADS):
+            at = (h * 4 + w) * HD
+            value_ref[at : at + HD] = window[h * HD : (h + 1) * HD]
+
+
 def block_kernel(
-    shift_lat_ref, shift_lon_ref, both_ref, far_ref, chip_ref, chip_far_ref, cross_ref,
-    cross_far_ref, attn_gain_ref, wk_ref, wq_t_ref, wv_t_ref, wproj_ref, mlp_gain_ref, wup_ref,
+    shift_ref, both_ref, chip_ref, chip_far_ref, cross_ref, cross_far_ref, score_ref, mark_ref,
+    query_ref, value_ref, attn_gain_ref, wk_ref, wv_t_ref, wproj_ref, mlp_gain_ref, wup_ref,
     wdown_ref, merge_gain_ref, wmerge_ref, out_ref,
 ):
     lat = lax.axis_index("lat")
     lev = lax.axis_index("lev")
-    last_lat = lax.axis_size("lat") - 1
-    shift_row = shift_lat_ref[0]
-    shift_col = shift_lon_ref[0]
-    _, row, col = token_coords(iota((TOK, 1), 0))
-    row_low = (row >= WH - shift_row).astype(jnp.int32)
-    col_low = (col >= WW - shift_col).astype(jnp.int32)
+    row_low, col_low = key_places(shift_ref)
     use_other = col_low == lev
-    use_chip = row_low == lat % 2
-    gain = row_of(attn_gain_ref)
-    own = both_ref[:TOK].astype(F32)
-    other = both_ref[TOK:].astype(F32)
-    chip_own = chip_ref[:TOK].astype(F32)
-    chip_other = chip_ref[TOK:].astype(F32)
-    cross_other = cross_ref[:TOK].astype(F32)
-    cross_own = cross_ref[TOK:].astype(F32)
-    beside = jnp.where(use_other, other, far_ref[...].astype(F32))
-    above = jnp.where(use_chip, chip_own, cross_own)
     corner = jnp.where(
-        use_chip,
-        jnp.where(use_other, chip_other, chip_far_ref[...].astype(F32)),
-        jnp.where(use_other, cross_other, cross_far_ref[...].astype(F32)),
-    )
-    own_n, beside_n, above_n, corner_n = [
-        layer_norm(x, gain) for x in (own, beside, above, corner)
+        row_low == lat % 2,
+        jnp.where(use_other, chip_ref[TOK:].astype(F32), chip_far_ref[...].astype(F32)),
+        jnp.where(use_other, cross_ref[:TOK].astype(F32), cross_far_ref[...].astype(F32)),
+    )
+    normed = layer_norm(corner, row_of(attn_gain_ref)).astype(BF16)
+    keys = dot(normed, wk_ref[...]).astype(BF16)
+    corner_values = dot_t(wv_t_ref[...], normed).astype(BF16)
+    _, lane_row, lane_col = token_coords(iota((1, TOK), 1))
+    lane_row, lane_col = shifted(lane_row, lane_col, shift_ref)
+    in_corner = [
+        ((lane_row != w // 2) & (lane_col != w % 2)).astype(F32).astype(BF16) for w in range(4)
     ]
-    windows = []
-    for a in range(2):
-        for b in range(2):
-            near = jnp.where(col_low == b, own_n, beside_n)
-            away = jnp.where(col_low == b, above_n, corner_n)
-            windows.append(jnp.where(row_low == a, near, away).astype(BF16))
-    keys = dot(jnp.concatenate(windows, axis=0), wk_ref[...]).astype(BF16)
-    values_t = [dot_t(wv_t_ref[...], x).astype(BF16) for x in windows]
-    query_t = dot_t(wq_t_ref[...], own_n.astype(BF16)).astype(BF16)
-
-    lanes = 256
-    per = lanes // HD
-    main = 128
-    rest = TOK - main
-    packed = per * TOK
-    lane = iota((1, packed), 1)
-    in_main = lane < per * main
-    token = jnp.where(in_main, split(lane, main)[1], main + split(lane, rest)[1])
-    _, token_row, token_col = token_coords(token)
-    label_row = (token_row >= WH - shift_row).astype(jnp.int32)
-    label = label_row * 2 + (token_col >= WW - shift_col).astype(jnp.int32)
-    outside = ((lat == 0) & (label_row == 0) & (row_low == 1)) | (
-        (lat == last_lat) & (label_row == 1) & (row_low == 0)
-    )
-    bias = jnp.where(outside, NEG_LARGE, 0.0)
-    head_of_row = split(iota((lanes, 1), 0), HD)[0]
-    rest_lane = iota((1, main), 1)
-    rest_head, rest_token = split(rest_lane, rest)
-    repeat = (iota((TOK, 1), 0) == main + rest_token).astype(F32).astype(BF16)
-    fold = (split(iota((main, 1), 0), rest)[1] == rest_lane).astype(F32).astype(BF16)
-    rest_mask = head_of_row == rest_head
-
+    label_row, label_col = query_places(shift_ref)
+    label = label_row * 2 + label_col
+    mark = mark_ref[...]
+    taken = mark <= 0.0
     def pick(parts, which):
         return jnp.where(
             which < 2,
@@ -229,38 +290,33 @@
             jnp.where(which == 2, parts[2], parts[3]),
         )
 
-    main_parts = []
-    rest_parts = []
-    for g in range(D // lanes):
-        lo = g * lanes
-        query_g = query_t[lo : lo + lanes]
-        query_main = query_g[:, :main].astype(F32)
-        blocks = [jnp.where(head_of_row == h, query_main, 0.0).astype(BF16) for h in range(per)]
-        blocks.append(jnp.where(rest_mask, dot(query_g, repeat), 0.0).astype(BF16))
-        scores_all = dot(keys[:, lo : lo + lanes], jnp.concatenate(blocks, axis=1))
-        scores = pick([scores_all[w * TOK : (w + 1) * TOK] for w in range(4)], label) + bias
+    label = jnp.concatenate([label[:, :MAIN], label[:, PER * MAIN : PER * MAIN + REST]], axis=1)
+    parts = []
+    for g in range(GROUPS):
+        lo = g * LANES
+        corner_scores = dot(keys[:, lo : lo + LANES], query_ref[lo : lo + LANES])
+        scores = jnp.where(taken, corner_scores + mark, score_ref[g])
         powers = jnp.exp2((scores - jnp.max(scores, axis=0, keepdims=True)) * (SCALE * LOG2E))
-        weights = (powers * (1.0 / jnp.sum(powers, axis=0, keepdims=True))).astype(BF16)
-        for h in range(per):
+        weights = powers * (1.0 / jnp.sum(powers, axis=0, keepdims=True))
+        rest = weights[:, PER * MAIN :]
+        for h in range(PER):
             at = lo + h * HD
-            stacked = jnp.concatenate([v[at : at + HD] for v in values_t], axis=0)
-            result = dot(stacked, weights[:, h * main : (h + 1) * main])
-            main_parts.append(
-                pick([result[w * HD : (w + 1) * HD] for w in range(4)], label[:, :main])
+            mine = corner_values[at : at + HD]
+            stack = value_ref[4 * at : 4 * (at + HD)] + jnp.concatenate(
+                [mine * m for m in in_corner], axis=0
             )
-        stacked = jnp.concatenate([v[lo : lo + lanes] for v in values_t], axis=0)
-        result = dot(stacked, weights[:, per * main :])
-        picked = pick([result[w * lanes : (w + 1) * lanes] for w in range(4)], label[:, per * main :])
-        rest_parts.append(dot(jnp.where(rest_mask, picked, 0.0).astype(BF16), fold))
-    window_out = jnp.concatenate(
-        [
-            jnp.concatenate(main_parts, axis=0).T,
-            jnp.concatenate(rest_parts, axis=0).T[:rest],
-        ],
-        axis=0,
-    ).astype(BF16)
-
-    middle = own + dot(window_out, wproj_ref[...])
+            tail = pltpu.roll(rest, MAIN - h * REST, 1) if h else rest
+            chosen = jnp.concatenate(
+                [weights[:, h * MAIN : (h + 1) * MAIN], tail[:, :REST]], axis=1
+            ).astype(BF16)
+            result = dot(stack, chosen)
+            parts.append(pick([result[w * HD : (w + 1) * HD] for w in range(4)], label))
+    window_out_t = jnp.concatenate(parts, axis=0).astype(BF16)
+
+    own = both_ref[:TOK].astype(F32)
+    middle = own + lax.dot_general(
+        window_out_t, wproj_ref[...], (((0,), (0,)), ((), ())), preferred_element_type=F32
+    )
     mlp_in = layer_norm(middle, row_of(mlp_gain_ref)).astype(BF16)
     up = dot(mlp_in, wup_ref[...])
     inner = math.sqrt(2.0 / math.pi) * (up + 0.044715 * (up * up * up))
@@ -357,7 +413,9 @@
     far_levels = lax.ppermute(levels_in, AXES, level_pairs)
     positions = levels_in.shape[0] * levels_in.shape[1] * levels_in.shape[2]
     kept = (w_kv, w_cross_out, w_proj, w_up, w_down, w_merge)
-    scores, values, query_rows, wq_t, wv_t, wk, wkv, wcross, wproj, wup, wdown, wmerge = pl.pallas_call(
+    (
+        scores, values, query_rows, wq_t, wv_t, wk, wkv, wcross, wproj, wup, wdown, wmerge, shifts,
+    ) = pl.pallas_call(
         local_kernel,
         out_shape=(
             pltpu.VMEM((positions, LATENT * HEADS), F32),
@@ -365,20 +423,29 @@
             pltpu.VMEM((LATENT * HEADS, D), BF16),
         )
         + (pltpu.VMEM((D, D), BF16),) * 3
-        + tuple(pltpu.VMEM(w.shape, BF16) for w in kept),
-        in_specs=[HBM_SPEC] + [VMEM_SPEC] * 2 + [HBM_SPEC] * 8,
-        out_specs=(VMEM_SPEC,) * 12,
+        + tuple(pltpu.VMEM(w.shape, BF16) for w in kept)
+        + (pltpu.VMEM((8, 128), jnp.int32),),
+        in_specs=[SMEM_SPEC] * 2 + [HBM_SPEC] * 11,
+        out_specs=(VMEM_SPEC,) * 13,
         scratch_shapes=[
+            pltpu.VMEM(enc_gain.shape, BF16),
+            pltpu.VMEM(latent_query.shape, BF16),
             pltpu.VMEM(levels_in.shape, BF16),
             pltpu.VMEM(w_query.shape, BF16),
             pltpu.VMEM(w_qkv.shape, BF16),
-            pltpu.SemaphoreType.DMA((9,)),
+            pltpu.SemaphoreType.DMA((11,)),
         ],
         compiler_params=params(14),
         name="local_levels",
     )(
-        in_hbm(levels_in), enc_gain, latent_query,
-        *[in_hbm(w) for w in (w_query, w_kv, w_qkv, w_cross_out, w_proj, w_up, w_down, w_merge)],
+        shift_lat, shift_lon,
+        *[
+            in_hbm(x)
+            for x in (
+                levels_in, enc_gain, latent_query, w_query, w_kv, w_qkv, w_cross_out, w_proj, w_up,
+                w_down, w_merge,
+            )
+        ]
     )
     both = pl.pallas_call(
         encode_kernel,
@@ -401,16 +468,29 @@
     far = lax.ppermute(other, AXES, far_pairs)
     cross_far = lax.ppermute(own, AXES, corner_pairs)
     chip_far = lax.ppermute(far, AXES, chip_pairs)
+    near, mark, query, value = pl.pallas_call(
+        near_kernel,
+        out_shape=(
+            pltpu.VMEM((GROUPS, TOK, PACKED), F32),
+            pltpu.VMEM((TOK, PACKED), F32),
+            pltpu.VMEM((D, PACKED), BF16),
+            pltpu.VMEM((4 * D, TOK), BF16),
+        ),
+        in_specs=[VMEM_SPEC] * 9,
+        out_specs=(VMEM_SPEC,) * 4,
+        compiler_params=params(14),
+        name="near_windows",
+    )(shifts, both, far, chip_both, cross_both, attn_gain, wk, wq_t, wv_t)
     merged = pl.pallas_call(
         block_kernel,
         out_shape=jax.ShapeDtypeStruct((WH // 2, WW // 2, LATENT, w_merge.shape[1]), BF16),
-        in_specs=[SMEM_SPEC] * 2 + [VMEM_SPEC] * 16,
+        in_specs=[VMEM_SPEC] * 19,
         out_specs=VMEM_SPEC,
-        compiler_params=params(24),
+        compiler_params=params(20),
         name="window_block",
     )(
-        shift_lat, shift_lon, both, far, chip_both, chip_far, cross_both, cross_far,
-        attn_gain, wk, wq_t, wv_t, wproj, mlp_gain, wup, wdown, merge_gain, wmerge,
+        shifts, both, chip_both, chip_far, cross_both, cross_far, near, mark, query, value,
+        attn_gain, wk, wv_t, wproj, mlp_gain, wup, wdown, merge_gain, wmerge,
     )
     return merged.transpose(2, 0, 1, 3)
 

time: 35.6 us -> 33.8 us (0.949)
  local copies, waits for them, and re-layouts: 1.38 us -> 0.03 us
  waiting for transfers between devices: 1.52 us -> 1.06 us
    pallas_call x1, Pallas kernels: 7.47 us -> 4.96 us  [on_device(): pl.pallas_call(block_kernel, out_shape=jax.ShapeDtypeStruct((WH // 2, WW...]
    pallas_call x0 -> x1, Pallas kernels: none -> 2.39 us  [on_device(): pl.pallas_call(near_kernel, out_shape=(pltpu.VMEM((GROUPS, TOK, PACKED),...]
    unnamed x10, local copies, waits for them, and re-layouts: 1.38 us -> 0.03 us
    ppermute x1, waiting for transfers between devices: 0.46 us -> 0.01 us  [on_device(): cross_far = lax.ppermute(own, AXES, corner_pairs)]
  transfers between devices with their start and end apart: 6 -> 6, of which waited for: 2 -> 1; matrix products, arithmetic and copies ran while one was open for 0% -> 0% of each run, Pallas kernels for 14% -> 22%
where the time goes in v4:
time: 33.8 us; the launch traced here: 33.7 us
  starting transfers between devices  17.1 us (51%)
  Pallas kernels  14.1 us (42%)
  between operations  1.43 us (4%)
  waiting for transfers between devices  1.06 us (3%)
    ppermute x1, starting transfers between devices, on_device(): cross_far = lax.ppermute(own, AXES, corner_pairs)  8.33 us
    pallas_call x1, Pallas kernels, on_device(): pl.pallas_call(block_kernel, out_shape=jax.ShapeDtypeStruct((WH // 2, WW...  4.96 us
    pallas_call x1, Pallas kernels, on_device(): pl.pallas_call(local_kernel, out_shape=(pltpu.VMEM((positions, LATENT * H...  4.9 us
    ppermute x1, starting transfers between devices, on_device(): cross_both = lax.ppermute(both, AXES, cross_pairs)  2.89 us
    pallas_call x1, Pallas kernels, on_device(): pl.pallas_call(near_kernel, out_shape=(pltpu.VMEM((GROUPS, TOK, PACKED),...  2.39 us
    ppermute x1, starting transfers between devices, on_device(): far_levels = lax.ppermute(levels_in, AXES, level_pairs)  2.13 us
    ppermute x1, starting transfers between devices, on_device(): chip_both = lax.ppermute(both, AXES, chip_pairs)  2 us
    pallas_call x1, Pallas kernels, on_device(): pl.pallas_call(encode_kernel, out_shape=jax.ShapeDtypeStruct((2 * TOK, D)...  1.83 us
  transfers between devices with their start and end apart: 6, of which 1 were waited for; matrix products, arithmetic and copies ran while one was open for 0% of the time, Pallas kernels for 22%

profile of v4, /device:TPU:1, one launch (start us, length us, event | category | flops | bytes accessed | tf_op | source)
XLA Modules:
  0.0 33.7 jit_solution(12606518434727218770)
XLA Ops:
  0.0 2.1 %collective-permute-start = (bf16[2,6,24,512]{3,2,1,0:T(8,128)(2,1)}, bf16[2,6,24,512]{3,2,1,0:T(8,128)(2,1)S(1)}, u32[]{:S(2)}, u32[]{:S(2)}) collective-permute-start(bf16[2,6,24,512]{3,2,1,0:T(8,128)(2,1)} %levels_hbm.1), channel_id=1, source_target_pairs={{0,1},{1,0},{2,3},{3,2},{4,5},{5,4},{6,7},{7,6},{8,9},{9,8},{10,11... | collective-permute-start | bytes 884744 | tf_op jit(solution)/shard_map/ppermute | solution.py:413
  3.4 0.0 copy-start
  3.4 0.0 copy-start.2
  3.4 4.9 %local_levels.1 = (f32[288,32]{1,0:T(8,128)S(1)}, bf16[288,512]{1,0:T(8,128)(2,1)S(1)}, bf16[32,512]{1,0:T(8,128)(2,1)S(1)}, bf16[512,512]{1,0:T(8,128)(2,1)S(1)...) custom-call(s32[1]{0:T(128)S(6)} %copy.17.shift_lat_ref, ...), custom_call_target="tpu_custom_call" | custom-call | tf_op jit(solution)/shard_map/local_levels/pallas_call | solution.py:418
  8.3 0.0 copy-start.3
  8.4 0.0 collective-permute-done.levels_ref
  8.4 0.0 copy-done
  8.4 0.0 copy-done.2
  8.4 1.8 %encode.1.both_ref = bf16[288,512]{1,0:T(8,128)(2,1)S(1)} custom-call(bf16[2,6,24,512]{3,2,1,0:T(8,128)(2,1)S(1)} %collective-permute-done.levels_ref, f32[288,32]{1,0:T(8,128)S(1)} %get-tuple-element.25.score_ref, bf16[288,512]{1,0:T(8,128)(2,1)S(1)} %get-tuple-element.26.value_ref, bf16[32,512]{1,0:T(8,128)(2,1)S(1)} %get-tuple-element.27.query_ref, ...), custom_call_target="tpu_custom_call" | custom-call | tf_op jit(solution)/shard_map/encode/pallas_call | solution.py:450
  10.2 0.0 copy-start.1
  10.2 0.0 copy-start.4
  10.2 2.0 %collective-permute-start.1 = (bf16[288,512]{1,0:T(8,128)(2,1)S(1)}, bf16[288,512]{1,0:T(8,128)(2,1)S(1)}, u32[]{:S(2)}, u32[]{:S(2)}) collective-permute-start(bf16[288,512]{1,0:T(8,128)(2,1)S(1)} %encode.1.both_ref), channel_id=1, source_target_pairs={{0,64},{1,65},{2,66},{3,67},{4,68},{5,69},{6,70},{7,71},{8,72},{9,... | collective-permute-start | bytes 884744 | tf_op jit(solution)/shard_map/ppermute | solution.py:458
  12.2 2.9 %collective-permute-start.4 = (bf16[288,512]{1,0:T(8,128)(2,1)S(1)}, bf16[288,512]{1,0:T(8,128)(2,1)S(1)}, u32[]{:S(2)}, u32[]{:S(2)}) collective-permute-start(bf16[288,512]{1,0:T(8,128)(2,1)S(1)} %encode.1.both_ref), channel_id=1, source_target_pairs={{0,1},{1,0},{2,3},{3,2},{4,5},{5,4},{6,7},{7,6},{8,9},{9,8},{10,11... | collective-permute-start | bytes 884744 | tf_op jit(solution)/shard_map/ppermute | solution.py:459
  15.1 0.0 collective-permute-done.1.chip_ref
  15.2 1.7 %collective-permute-start.2 = (bf16[144,512]{1,0:T(8,128)(2,1)S(1)}, bf16[144,512]{1,0:T(8,128)(2,1)S(1)}, u32[]{:S(2)}, u32[]{:S(2)}) collective-permute-start(bf16[144,512]{1,0:T(8,128)(2,1)S(1)} %get-tuple-element.30), channel_id=1, source_target_pairs={{0,2},{1,63},{2,4},{3,1},{4,6},{5,3},{6,8},{7,5},{8,10},{9,7},{10,... | collective-permute-start | bytes 442376 | tf_op jit(solution)/shard_map/ppermute | solution.py:468
  16.9 8.3 %collective-permute-start.5 = (bf16[144,512]{1,0:T(8,128)(2,1)S(1)}, bf16[144,512]{1,0:T(8,128)(2,1)S(1)}, u32[]{:S(2)}, u32[]{:S(2)}) collective-permute-start(bf16[144,512]{1,0:T(8,128)(2,1)S(1)} %get-tuple-element.31), channel_id=1, source_target_pairs={{0,1},{1,0},{2,3},{3,2},{4,5},{5,4},{6,7},{7,6},{8,9},{9,8},{10,11... | collective-permute-start | bytes 442376 | tf_op jit(solution)/shard_map/ppermute | solution.py:469
  25.2 1.0 %collective-permute-done.2.far_ref = bf16[144,512]{1,0:T(8,128)(2,1)S(1)} collective-permute-done((bf16[144,512]{1,0:T(8,128)(2,1)S(1)}, bf16[144,512]{1,0:T(8,128)(2,1)S(1)}, u32[]{:S(2)}, u32[]{:S(2)}) %collective-permute-start.2) | collective-permute-done | bytes 147488 | tf_op jit(solution)/shard_map/ppermute | solution.py:468
  26.3 0.0 collective-permute-start.3
  26.3 0.0 collective-permute-done.4.cross_ref
  26.3 0.0 copy-done.3
  26.3 2.4 %near_windows.1 = (f32[2,144,1152]{2,1,0:T(8,128)S(1)}, f32[144,1152]{1,0:T(8,128)S(1)}, bf16[512,1152]{1,0:T(8,128)(2,1)S(1)}, bf16[2048,144]{1,0:T(8,128)(2,1)S(1)}) custom-call(s32[8,128]{1,0:T(8,128)S(1)} %get-tuple-element.24.shift_ref, bf16[288,512]{1,0:T(8,128)(2,1)S(1)} %encode.1.both_ref, bf16[144,512]{1,0:T(8,128)(2,1)S(1)} %collective-permute-done.2.far_ref, ...), custom_call_target="tpu_custom_call" | custom-call | tf_op jit(solution)/shard_map/near_windows/pallas_call | solution.py:471
  28.7 0.0 collective-permute-done.5.cross_far_ref
  28.7 0.0 collective-permute-done.3.chip_far_ref
  28.7 0.0 copy-done.1
  28.7 0.0 copy-done.4
  28.7 5.0 %window_block.1 = bf16[3,6,2,1024]{3,2,1,0:T(2,128)(2,1)} custom-call(s32[8,128]{1,0:T(8,128)S(1)} %get-tuple-element.24.shift_ref, bf16[288,512]{1,0:T(8,128)(2,1)S(1)} %encode.1.both_ref, bf16[288,512]{1,0:T(8,128)(2,1)S(1)} %collective-permute-done.1.chip_ref, bf16[144,512]{1,0:T(8,128)(2,1)S(1)} %collective-permute-done.3.chip_far_ref, ...), custom_call_target="tpu_custom_call" | custom-call | tf_op jit(solution)/shard_map/window_block/pallas_call | solution.py:484
  (1 shorter events, 0.0 us)
Async XLA Ops:
  0.0 8.4 %collective-permute-start = (bf16[2,6,24,512]{3,2,1,0:T(8,128)(2,1)}, bf16[2,6,24,512]{3,2,1,0:T(8,128)(2,1)S(1)}, u32[]{:S(2)}, u32[]{:S(2)}) collective-permute-start(bf16[2,6,24,512]{3,2,1,0:T(8,128)(2,1)} %levels_hbm.1), channel_id=1, source_target_pairs={{0,1},{1,0},{2,3},{3,2},{4,5},{5,4},{6,7},{7,6},{8,9},{9,8},{10,11... | collective-permute-start | bytes 884744 | tf_op jit(solution)/shard_map/ppermute | solution.py:413
  3.4 4.9 %copy-start = (bf16[2,512]{1,0:T(2,128)(2,1)S(1)}, bf16[2,512]{1,0:T(2,128)(2,1)}, u32[]{:S(2)}) copy-start(bf16[2,512]{1,0:T(2,128)(2,1)} %lq_ref.1) | copy-start | bytes 6148
  3.4 4.9 %copy-start.2 = (bf16[512]{0:T(512)(128)(2,1)S(1)}, bf16[512]{0:T(512)(128)(2,1)}, u32[]{:S(2)}) copy-start(bf16[512]{0:T(512)(128)(2,1)} %gain_ref.2) | copy-start | bytes 3076
  8.3 17.9 %copy-start.3 = (bf16[512]{0:T(512)(128)(2,1)S(1)}, bf16[512]{0:T(512)(128)(2,1)}, u32[]{:S(2)}) copy-start(bf16[512]{0:T(512)(128)(2,1)} %attn_gain_ref.1) | copy-start | bytes 3076
  10.2 18.5 %copy-start.1 = (bf16[2048]{0:T(1024)(128)(2,1)S(1)}, bf16[2048]{0:T(1024)(128)(2,1)}, u32[]{:S(2)}) copy-start(bf16[2048]{0:T(1024)(128)(2,1)} %merge_gain_ref.1) | copy-start | bytes 12292
  10.2 18.5 %copy-start.4 = (bf16[512]{0:T(512)(128)(2,1)S(1)}, bf16[512]{0:T(512)(128)(2,1)}, u32[]{:S(2)}) copy-start(bf16[512]{0:T(512)(128)(2,1)} %mlp_gain_ref.1) | copy-start | bytes 3076
  10.2 4.9 %collective-permute-start.1 = (bf16[288,512]{1,0:T(8,128)(2,1)S(1)}, bf16[288,512]{1,0:T(8,128)(2,1)S(1)}, u32[]{:S(2)}, u32[]{:S(2)}) collective-permute-start(bf16[288,512]{1,0:T(8,128)(2,1)S(1)} %encode.1.both_ref), channel_id=1, source_target_pairs={{0,64},{1,65},{2,66},{3,67},{4,68},{5,69},{6,70},{7,71},{8,72},{9,... | collective-permute-start | bytes 884744 | tf_op jit(solution)/shard_map/ppermute | solution.py:458
  12.2 14.0 %collective-permute-start.4 = (bf16[288,512]{1,0:T(8,128)(2,1)S(1)}, bf16[288,512]{1,0:T(8,128)(2,1)S(1)}, u32[]{:S(2)}, u32[]{:S(2)}) collective-permute-start(bf16[288,512]{1,0:T(8,128)(2,1)S(1)} %encode.1.both_ref), channel_id=1, source_target_pairs={{0,1},{1,0},{2,3},{3,2},{4,5},{5,4},{6,7},{7,6},{8,9},{9,8},{10,11... | collective-permute-start | bytes 884744 | tf_op jit(solution)/shard_map/ppermute | solution.py:459
  15.2 11.1 %collective-permute-start.2 = (bf16[144,512]{1,0:T(8,128)(2,1)S(1)}, bf16[144,512]{1,0:T(8,128)(2,1)S(1)}, u32[]{:S(2)}, u32[]{:S(2)}) collective-permute-start(bf16[144,512]{1,0:T(8,128)(2,1)S(1)} %get-tuple-element.30), channel_id=1, source_target_pairs={{0,2},{1,63},{2,4},{3,1},{4,6},{5,3},{6,8},{7,5},{8,10},{9,7},{10,... | collective-permute-start | bytes 442376 | tf_op jit(solution)/shard_map/ppermute | solution.py:468
  16.9 11.8 %collective-permute-start.5 = (bf16[144,512]{1,0:T(8,128)(2,1)S(1)}, bf16[144,512]{1,0:T(8,128)(2,1)S(1)}, u32[]{:S(2)}, u32[]{:S(2)}) collective-permute-start(bf16[144,512]{1,0:T(8,128)(2,1)S(1)} %get-tuple-element.31), channel_id=1, source_target_pairs={{0,1},{1,0},{2,3},{3,2},{4,5},{5,4},{6,7},{7,6},{8,9},{9,8},{10,11... | collective-permute-start | bytes 442376 | tf_op jit(solution)/shard_map/ppermute | solution.py:469
  26.3 2.4 %collective-permute-start.3 = (bf16[144,512]{1,0:T(8,128)(2,1)S(1)}, bf16[144,512]{1,0:T(8,128)(2,1)S(1)}, u32[]{:S(2)}, u32[]{:S(2)}) collective-permute-start(bf16[144,512]{1,0:T(8,128)(2,1)S(1)} %collective-permute-done.2.far_ref), channel_id=1, source_target_pairs={{0,64},{1,65},{2,66},{3,67},{4,68},{5,69},{6,70},{7,71},{8,72},{9,... | collective-permute-start | bytes 442376 | tf_op jit(solution)/shard_map/ppermute | solution.py:470

commit v5 on v4

--- a/solution.py
+++ b/solution.py
@@ -47,9 +47,31 @@
 
 
 def token_coords(index):
-    level, rest = split(index, WH * WW)
-    row, col = split(rest, WW)
-    return level, row, col
+    pair, place = split(index, 2 * WW)
+    level, pair = split(pair, WH // 2)
+    odd = jnp.where(place < 16, place >> 3, (place >> 2) & 1)
+    col = jnp.where(place < 16, place & 7, 8 + (place & 3))
+    return level, 2 * pair + odd, col
+
+
+def token_index(level, pair, odd, col):
+    place = jnp.where(col < 8, odd * 8 + col, 8 + odd * 4 + col)
+    return (level * (WH // 2) + pair) * (2 * WW) + place
+
+
+def halves_of(latents):
+    upper = iota((8, 1), 0) < 4
+    left, right = [], []
+    for start in range(0, latents.shape[0], 4 * WW):
+        tiles = [latents[start + 8 * i : start + 8 * i + 8] for i in range(6)]
+        turned = [pltpu.roll(tiles[i], 4, 0) if i % 3 else None for i in range(6)]
+        left += [tiles[0], tiles[3], jnp.where(upper, tiles[1], turned[4])]
+        right += [
+            jnp.where(upper, turned[1], turned[2]),
+            jnp.where(upper, turned[4], turned[5]),
+            jnp.where(upper, turned[2], tiles[5]),
+        ]
+    return jnp.concatenate(left, axis=0), jnp.concatenate(right, axis=0)
 
 
 def row_of(ref):
@@ -146,13 +168,12 @@
     query = lq_ref[...].astype(F32)
     latents = jnp.concatenate(
         [projected[k * count : (k + 1) * count] + query[k : k + 1] for k in range(LATENT)], axis=0
+    )
+    left, right = halves_of(latents)
+    first = lev == 0
+    both = jnp.concatenate(
+        [jnp.where(first, left, right), jnp.where(first, right, left)], axis=0
     ).astype(BF16)
-    half, rest = split(iota((2 * TOK, 1), 0), TOK)
-    level, row, col = token_coords(rest)
-    side = jnp.where(half == 0, lev, 1 - lev)
-    source = level * count + row * (2 * WW) + col + side * WW
-    order = (iota((1, 2 * TOK), 1) == source).astype(F32).astype(BF16)
-    both = dot(order, latents).astype(BF16)
     both_ref[...] = both
 
 
@@ -242,16 +263,15 @@
     _, lane_row, lane_col = token_coords(iota((1, TOK), 1))
     lane_row, lane_col = shifted(lane_row, lane_col, shift_ref)
     values = [
-        dot_t(wv_t_ref[...], normed[i * TOK : (i + 1) * TOK]) for i in range(3)
+        dot_t(wv_t_ref[...], normed[i * TOK : (i + 1) * TOK]).astype(BF16) for i in range(3)
     ]
     for w in range(4):
         in_row = lane_row == w // 2
         in_col = lane_col == w % 2
-        window = jnp.where(
-            in_row,
-            jnp.where(in_col, values[0], values[1]),
-            jnp.where(in_col, values[2], 0.0),
-        ).astype(BF16)
+        masks = [
+            x.astype(F32).astype(BF16) for x in (in_row & in_col, in_row & ~in_col, ~in_row & in_col)
+        ]
+        window = values[0] * masks[0] + values[1] * masks[1] + values[2] * masks[2]
         for h in range(HEADS):
             at = (h * 4 + w) * HD
             value_ref[at : at + HD] = window[h * HD : (h + 1) * HD]
@@ -329,7 +349,7 @@
     pair, level = split(place, LATENT)
     row_pair, col_pair = split(pair, WW // 2)
     corner_col, corner_row = split(corner_index, 2)
-    source = level * (WH * WW) + (row_pair * 2 + corner_row) * WW + col_pair * 2 + corner_col
+    source = token_index(level, row_pair, corner_row, col_pair * 2 + corner_col)
     source = jnp.where(place < count, source, -1)
     order = (iota((1, TOK), 1) == source).astype(F32).astype(BF16)
     sorted_out = dot(order, block_out)

time: 33.8 us -> 33.5 us (level)
    pallas_call x1, Pallas kernels: 1.83 us -> 1.47 us  [on_device(): pl.pallas_call(encode_kernel, out_shape=jax.ShapeDtypeStruct((2 * TOK, D)...]
where the time goes in v5:
time: 33.5 us; the launch traced here: 33.4 us
  starting transfers between devices  17.1 us (51%)
  Pallas kernels  13.8 us (41%)
  between operations  1.43 us (4%)
  waiting for transfers between devices  1.06 us (3%)
    ppermute x1, starting transfers between devices, on_device(): cross_far = lax.ppermute(own, AXES, corner_pairs)  8.33 us
    pallas_call x1, Pallas kernels, on_device(): pl.pallas_call(block_kernel, out_shape=jax.ShapeDtypeStruct((WH // 2, WW...  4.98 us
    pallas_call x1, Pallas kernels, on_device(): pl.pallas_call(local_kernel, out_shape=(pltpu.VMEM((positions, LATENT * H...  4.9 us
    ppermute x1, starting transfers between devices, on_device(): cross_both = lax.ppermute(both, AXES, cross_pairs)  2.89 us
    pallas_call x1, Pallas kernels, on_device(): pl.pallas_call(near_kernel, out_shape=(pltpu.VMEM((GROUPS, TOK, PACKED),...  2.45 us
    ppermute x1, starting transfers between devices, on_device(): far_levels = lax.ppermute(levels_in, AXES, level_pairs)  2.13 us
    ppermute x1, starting transfers between devices, on_device(): chip_both = lax.ppermute(both, AXES, chip_pairs)  2 us
    ppermute x1, starting transfers between devices, on_device(): far = lax.ppermute(other, AXES, far_pairs)  1.72 us
  transfers between devices with their start and end apart: 6, of which 1 were waited for; matrix products, arithmetic and copies ran while one was open for 0% of the time, Pallas kernels for 22%

profile of v5, /device:TPU:1, one launch (start us, length us, event | category | flops | bytes accessed | tf_op | source)
XLA Modules:
  0.0 33.4 jit_solution(11905415545664403590)
XLA Ops:
  0.0 2.1 %collective-permute-start = (bf16[2,6,24,512]{3,2,1,0:T(8,128)(2,1)}, bf16[2,6,24,512]{3,2,1,0:T(8,128)(2,1)S(1)}, u32[]{:S(2)}, u32[]{:S(2)}) collective-permute-start(bf16[2,6,24,512]{3,2,1,0:T(8,128)(2,1)} %levels_hbm.1), channel_id=1, source_target_pairs={{0,1},{1,0},{2,3},{3,2},{4,5},{5,4},{6,7},{7,6},{8,9},{9,8},{10,11... | collective-permute-start | bytes 884744 | tf_op jit(solution)/shard_map/ppermute | solution.py:433
  3.4 0.0 copy-start
  3.4 0.0 copy-start.2
  3.4 4.9 %local_levels.1 = (f32[288,32]{1,0:T(8,128)S(1)}, bf16[288,512]{1,0:T(8,128)(2,1)S(1)}, bf16[32,512]{1,0:T(8,128)(2,1)S(1)}, bf16[512,512]{1,0:T(8,128)(2,1)S(1)...) custom-call(s32[1]{0:T(128)S(6)} %copy.17.shift_lat_ref, ...), custom_call_target="tpu_custom_call" | custom-call | tf_op jit(solution)/shard_map/local_levels/pallas_call | solution.py:438
  8.3 0.0 copy-start.3
  8.4 0.0 collective-permute-done.levels_ref
  8.4 0.0 copy-done
  8.4 0.0 copy-done.2
  8.4 1.5 %encode.1.both_ref = bf16[288,512]{1,0:T(8,128)(2,1)S(1)} custom-call(bf16[2,6,24,512]{3,2,1,0:T(8,128)(2,1)S(1)} %collective-permute-done.levels_ref, f32[288,32]{1,0:T(8,128)S(1)} %get-tuple-element.25.score_ref, bf16[288,512]{1,0:T(8,128)(2,1)S(1)} %get-tuple-element.26.value_ref, bf16[32,512]{1,0:T(8,128)(2,1)S(1)} %get-tuple-element.27.query_ref, ...), custom_call_target="tpu_custom_call" | custom-call | tf_op jit(solution)/shard_map/encode/pallas_call | solution.py:470
  9.9 0.0 copy-start.1
  9.9 0.0 copy-start.4
  9.9 2.0 %collective-permute-start.1 = (bf16[288,512]{1,0:T(8,128)(2,1)S(1)}, bf16[288,512]{1,0:T(8,128)(2,1)S(1)}, u32[]{:S(2)}, u32[]{:S(2)}) collective-permute-start(bf16[288,512]{1,0:T(8,128)(2,1)S(1)} %encode.1.both_ref), channel_id=1, source_target_pairs={{0,64},{1,65},{2,66},{3,67},{4,68},{5,69},{6,70},{7,71},{8,72},{9,... | collective-permute-start | bytes 884744 | tf_op jit(solution)/shard_map/ppermute | solution.py:478
  11.9 2.9 %collective-permute-start.4 = (bf16[288,512]{1,0:T(8,128)(2,1)S(1)}, bf16[288,512]{1,0:T(8,128)(2,1)S(1)}, u32[]{:S(2)}, u32[]{:S(2)}) collective-permute-start(bf16[288,512]{1,0:T(8,128)(2,1)S(1)} %encode.1.both_ref), channel_id=1, source_target_pairs={{0,1},{1,0},{2,3},{3,2},{4,5},{5,4},{6,7},{7,6},{8,9},{9,8},{10,11... | collective-permute-start | bytes 884744 | tf_op jit(solution)/shard_map/ppermute | solution.py:479
  14.8 0.0 collective-permute-done.1.chip_ref
  14.8 1.7 %collective-permute-start.2 = (bf16[144,512]{1,0:T(8,128)(2,1)S(1)}, bf16[144,512]{1,0:T(8,128)(2,1)S(1)}, u32[]{:S(2)}, u32[]{:S(2)}) collective-permute-start(bf16[144,512]{1,0:T(8,128)(2,1)S(1)} %get-tuple-element.30), channel_id=1, source_target_pairs={{0,2},{1,63},{2,4},{3,1},{4,6},{5,3},{6,8},{7,5},{8,10},{9,7},{10,... | collective-permute-start | bytes 442376 | tf_op jit(solution)/shard_map/ppermute | solution.py:488
  16.5 8.3 %collective-permute-start.5 = (bf16[144,512]{1,0:T(8,128)(2,1)S(1)}, bf16[144,512]{1,0:T(8,128)(2,1)S(1)}, u32[]{:S(2)}, u32[]{:S(2)}) collective-permute-start(bf16[144,512]{1,0:T(8,128)(2,1)S(1)} %get-tuple-element.31), channel_id=1, source_target_pairs={{0,1},{1,0},{2,3},{3,2},{4,5},{5,4},{6,7},{7,6},{8,9},{9,8},{10,11... | collective-permute-start | bytes 442376 | tf_op jit(solution)/shard_map/ppermute | solution.py:489
  24.9 1.0 %collective-permute-done.2.far_ref = bf16[144,512]{1,0:T(8,128)(2,1)S(1)} collective-permute-done((bf16[144,512]{1,0:T(8,128)(2,1)S(1)}, bf16[144,512]{1,0:T(8,128)(2,1)S(1)}, u32[]{:S(2)}, u32[]{:S(2)}) %collective-permute-start.2) | collective-permute-done | bytes 147488 | tf_op jit(solution)/shard_map/ppermute | solution.py:488
  25.9 0.0 collective-permute-start.3
  25.9 0.0 collective-permute-done.4.cross_ref
  25.9 0.0 copy-done.3
  25.9 2.5 %near_windows.1 = (f32[2,144,1152]{2,1,0:T(8,128)S(1)}, f32[144,1152]{1,0:T(8,128)S(1)}, bf16[512,1152]{1,0:T(8,128)(2,1)S(1)}, bf16[2048,144]{1,0:T(8,128)(2,1)S(1)}) custom-call(s32[8,128]{1,0:T(8,128)S(1)} %get-tuple-element.24.shift_ref, bf16[288,512]{1,0:T(8,128)(2,1)S(1)} %encode.1.both_ref, bf16[144,512]{1,0:T(8,128)(2,1)S(1)} %collective-permute-done.2.far_ref, ...), custom_call_target="tpu_custom_call" | custom-call | tf_op jit(solution)/shard_map/near_windows/pallas_call | solution.py:491
  28.4 0.0 collective-permute-done.5.cross_far_ref
  28.4 0.0 collective-permute-done.3.chip_far_ref
  28.4 0.0 copy-done.1
  28.4 0.0 copy-done.4
  28.4 5.0 %window_block.1 = bf16[3,6,2,1024]{3,2,1,0:T(2,128)(2,1)} custom-call(s32[8,128]{1,0:T(8,128)S(1)} %get-tuple-element.24.shift_ref, bf16[288,512]{1,0:T(8,128)(2,1)S(1)} %encode.1.both_ref, bf16[288,512]{1,0:T(8,128)(2,1)S(1)} %collective-permute-done.1.chip_ref, bf16[144,512]{1,0:T(8,128)(2,1)S(1)} %collective-permute-done.3.chip_far_ref, ...), custom_call_target="tpu_custom_call" | custom-call | tf_op jit(solution)/shard_map/window_block/pallas_call | solution.py:504
  (1 shorter events, 0.0 us)
Async XLA Ops:
  0.0 8.4 %collective-permute-start = (bf16[2,6,24,512]{3,2,1,0:T(8,128)(2,1)}, bf16[2,6,24,512]{3,2,1,0:T(8,128)(2,1)S(1)}, u32[]{:S(2)}, u32[]{:S(2)}) collective-permute-start(bf16[2,6,24,512]{3,2,1,0:T(8,128)(2,1)} %levels_hbm.1), channel_id=1, source_target_pairs={{0,1},{1,0},{2,3},{3,2},{4,5},{5,4},{6,7},{7,6},{8,9},{9,8},{10,11... | collective-permute-start | bytes 884744 | tf_op jit(solution)/shard_map/ppermute | solution.py:433
  3.4 4.9 %copy-start = (bf16[2,512]{1,0:T(2,128)(2,1)S(1)}, bf16[2,512]{1,0:T(2,128)(2,1)}, u32[]{:S(2)}) copy-start(bf16[2,512]{1,0:T(2,128)(2,1)} %lq_ref.1) | copy-start | bytes 6148
  3.4 4.9 %copy-start.2 = (bf16[512]{0:T(512)(128)(2,1)S(1)}, bf16[512]{0:T(512)(128)(2,1)}, u32[]{:S(2)}) copy-start(bf16[512]{0:T(512)(128)(2,1)} %gain_ref.2) | copy-start | bytes 3076
  8.3 17.6 %copy-start.3 = (bf16[512]{0:T(512)(128)(2,1)S(1)}, bf16[512]{0:T(512)(128)(2,1)}, u32[]{:S(2)}) copy-start(bf16[512]{0:T(512)(128)(2,1)} %attn_gain_ref.1) | copy-start | bytes 3076
  9.9 18.5 %copy-start.1 = (bf16[2048]{0:T(1024)(128)(2,1)S(1)}, bf16[2048]{0:T(1024)(128)(2,1)}, u32[]{:S(2)}) copy-start(bf16[2048]{0:T(1024)(128)(2,1)} %merge_gain_ref.1) | copy-start | bytes 12292
  9.9 18.5 %copy-start.4 = (bf16[512]{0:T(512)(128)(2,1)S(1)}, bf16[512]{0:T(512)(128)(2,1)}, u32[]{:S(2)}) copy-start(bf16[512]{0:T(512)(128)(2,1)} %mlp_gain_ref.1) | copy-start | bytes 3076
  9.9 4.9 %collective-permute-start.1 = (bf16[288,512]{1,0:T(8,128)(2,1)S(1)}, bf16[288,512]{1,0:T(8,128)(2,1)S(1)}, u32[]{:S(2)}, u32[]{:S(2)}) collective-permute-start(bf16[288,512]{1,0:T(8,128)(2,1)S(1)} %encode.1.both_ref), channel_id=1, source_target_pairs={{0,64},{1,65},{2,66},{3,67},{4,68},{5,69},{6,70},{7,71},{8,72},{9,... | collective-permute-start | bytes 884744 | tf_op jit(solution)/shard_map/ppermute | solution.py:478
  11.9 14.0 %collective-permute-start.4 = (bf16[288,512]{1,0:T(8,128)(2,1)S(1)}, bf16[288,512]{1,0:T(8,128)(2,1)S(1)}, u32[]{:S(2)}, u32[]{:S(2)}) collective-permute-start(bf16[288,512]{1,0:T(8,128)(2,1)S(1)} %encode.1.both_ref), channel_id=1, source_target_pairs={{0,1},{1,0},{2,3},{3,2},{4,5},{5,4},{6,7},{7,6},{8,9},{9,8},{10,11... | collective-permute-start | bytes 884744 | tf_op jit(solution)/shard_map/ppermute | solution.py:479
  14.8 11.1 %collective-permute-start.2 = (bf16[144,512]{1,0:T(8,128)(2,1)S(1)}, bf16[144,512]{1,0:T(8,128)(2,1)S(1)}, u32[]{:S(2)}, u32[]{:S(2)}) collective-permute-start(bf16[144,512]{1,0:T(8,128)(2,1)S(1)} %get-tuple-element.30), channel_id=1, source_target_pairs={{0,2},{1,63},{2,4},{3,1},{4,6},{5,3},{6,8},{7,5},{8,10},{9,7},{10,... | collective-permute-start | bytes 442376 | tf_op jit(solution)/shard_map/ppermute | solution.py:488
  16.5 11.9 %collective-permute-start.5 = (bf16[144,512]{1,0:T(8,128)(2,1)S(1)}, bf16[144,512]{1,0:T(8,128)(2,1)S(1)}, u32[]{:S(2)}, u32[]{:S(2)}) collective-permute-start(bf16[144,512]{1,0:T(8,128)(2,1)S(1)} %get-tuple-element.31), channel_id=1, source_target_pairs={{0,1},{1,0},{2,3},{3,2},{4,5},{5,4},{6,7},{7,6},{8,9},{9,8},{10,11... | collective-permute-start | bytes 442376 | tf_op jit(solution)/shard_map/ppermute | solution.py:489
  25.9 2.5 %collective-permute-start.3 = (bf16[144,512]{1,0:T(8,128)(2,1)S(1)}, bf16[144,512]{1,0:T(8,128)(2,1)S(1)}, u32[]{:S(2)}, u32[]{:S(2)}) collective-permute-start(bf16[144,512]{1,0:T(8,128)(2,1)S(1)} %collective-permute-done.2.far_ref), channel_id=1, source_target_pairs={{0,64},{1,65},{2,66},{3,67},{4,68},{5,69},{6,70},{7,71},{8,72},{9,... | collective-permute-start | bytes 442376 | tf_op jit(solution)/shard_map/ppermute | solution.py:490

commit v6 on v5

--- a/solution.py
+++ b/solution.py
@@ -216,20 +216,18 @@
     return head, token, split(iota((LANES, 1), 0), HD)[0] == head
 
 
-def near_kernel(
-    shift_ref, both_ref, far_ref, chip_ref, cross_ref, gain_ref, wk_ref, wq_t_ref, wv_t_ref,
+def early_kernel(
+    shift_ref, both_ref, chip_ref, cross_ref, gain_ref, wk_ref, wq_t_ref, wv_t_ref,
     score_ref, mark_ref, query_ref, value_ref,
 ):
     lat = lax.axis_index("lat")
-    lev = lax.axis_index("lev")
     last_lat = lax.axis_size("lat") - 1
     row_low, col_low = key_places(shift_ref)
     own = both_ref[:TOK].astype(F32)
-    beside = jnp.where(col_low == lev, both_ref[TOK:].astype(F32), far_ref[...].astype(F32))
     above = jnp.where(
         row_low == lat % 2, chip_ref[:TOK].astype(F32), cross_ref[TOK:].astype(F32)
     )
-    tokens = jnp.concatenate([own, beside, above], axis=0)
+    tokens = jnp.concatenate([own, above], axis=0)
     normed = layer_norm(tokens, row_of(gain_ref)).astype(BF16)
     keys = dot(normed, wk_ref[...]).astype(BF16)
     query_t = dot_t(wq_t_ref[...], normed[:TOK]).astype(BF16)
@@ -241,7 +239,7 @@
         ((lat == 0) & (row_low == 1)) | ((lat == last_lat) & (row_low == 0))
     )
     bias = jnp.where(outside, NEG_LARGE, 0.0)
-    mark_ref[...] = jnp.where(same_row | same_col, 1.0, bias)
+    mark_ref[...] = jnp.where(same_col, 1.0, jnp.where(same_row, 2.0, bias))
     _, rest_token, rest_mask = rest_places()
     head_of_row = split(iota((LANES, 1), 0), HD)[0]
     repeat = (iota((TOK, 1), 0) == MAIN + rest_token).astype(F32).astype(BF16)
@@ -254,27 +252,50 @@
         packed = jnp.concatenate(blocks, axis=1)
         query_ref[lo : lo + LANES] = packed
         scores = dot(keys[:, lo : lo + LANES], packed)
-        score_ref[g] = bias + jnp.where(
-            same_row,
-            jnp.where(same_col, scores[:TOK], scores[TOK : 2 * TOK]),
-            scores[2 * TOK :],
-        )
+        score_ref[g] = bias + jnp.where(same_row, scores[:TOK], scores[TOK:])
 
     _, lane_row, lane_col = token_coords(iota((1, TOK), 1))
     lane_row, lane_col = shifted(lane_row, lane_col, shift_ref)
     values = [
-        dot_t(wv_t_ref[...], normed[i * TOK : (i + 1) * TOK]).astype(BF16) for i in range(3)
+        dot_t(wv_t_ref[...], normed[i * TOK : (i + 1) * TOK]) for i in range(2)
     ]
     for w in range(4):
-        in_row = lane_row == w // 2
-        in_col = lane_col == w % 2
-        masks = [
-            x.astype(F32).astype(BF16) for x in (in_row & in_col, in_row & ~in_col, ~in_row & in_col)
-        ]
-        window = values[0] * masks[0] + values[1] * masks[1] + values[2] * masks[2]
+        window = jnp.where(lane_row == w // 2, values[0], values[1])
+        window = jnp.where(lane_col == w % 2, window, 0.0).astype(BF16)
         for h in range(HEADS):
             at = (h * 4 + w) * HD
             value_ref[at : at + HD] = window[h * HD : (h + 1) * HD]
+
+
+def relay_kernel(far_ref, mark_ref, out_ref):
+    out_ref[...] = far_ref[...]
+
+
+def beside_kernel(
+    shift_ref, both_ref, far_ref, score_in_ref, mark_ref, query_ref, value_in_ref, gain_ref,
+    wk_ref, wv_t_ref, score_ref, value_ref,
+):
+    lev = lax.axis_index("lev")
+    _, col_low = key_places(shift_ref)
+    beside = jnp.where(col_low == lev, both_ref[TOK:].astype(F32), far_ref[...].astype(F32))
+    normed = layer_norm(beside, row_of(gain_ref)).astype(BF16)
+    keys = dot(normed, wk_ref[...]).astype(BF16)
+    taken = mark_ref[...] == 2.0
+    for g in range(GROUPS):
+        lo = g * LANES
+        scores = dot(keys[:, lo : lo + LANES], query_ref[lo : lo + LANES])
+        score_ref[g] = jnp.where(taken, scores, score_in_ref[g])
+    values = dot_t(wv_t_ref[...], normed).astype(BF16)
+    _, lane_row, lane_col = token_coords(iota((1, TOK), 1))
+    lane_row, lane_col = shifted(lane_row, lane_col, shift_ref)
+    masks = [
+        ((lane_row == w // 2) & (lane_col != w % 2)).astype(F32).astype(BF16) for w in range(4)
+    ]
+    for h in range(HEADS):
+        mine = values[h * HD : (h + 1) * HD]
+        for w in range(4):
+            at = (h * 4 + w) * HD
+            value_ref[at : at + HD] = value_in_ref[at : at + HD] + mine * masks[w]
 
 
 def block_kernel(
@@ -487,20 +508,38 @@
     )(both, chip_both)
     far = lax.ppermute(other, AXES, far_pairs)
     cross_far = lax.ppermute(own, AXES, corner_pairs)
-    chip_far = lax.ppermute(far, AXES, chip_pairs)
-    near, mark, query, value = pl.pallas_call(
-        near_kernel,
+    score_type = pltpu.VMEM((GROUPS, TOK, PACKED), F32)
+    value_type = pltpu.VMEM((4 * D, TOK), BF16)
+    early, mark, query, early_value = pl.pallas_call(
+        early_kernel,
         out_shape=(
-            pltpu.VMEM((GROUPS, TOK, PACKED), F32),
+            score_type,
             pltpu.VMEM((TOK, PACKED), F32),
             pltpu.VMEM((D, PACKED), BF16),
-            pltpu.VMEM((4 * D, TOK), BF16),
+            value_type,
         ),
-        in_specs=[VMEM_SPEC] * 9,
+        in_specs=[VMEM_SPEC] * 8,
         out_specs=(VMEM_SPEC,) * 4,
         compiler_params=params(14),
-        name="near_windows",
-    )(shifts, both, far, chip_both, cross_both, attn_gain, wk, wq_t, wv_t)
+        name="early_windows",
+    )(shifts, both, chip_both, cross_both, attn_gain, wk, wq_t, wv_t)
+    far = pl.pallas_call(
+        relay_kernel,
+        out_shape=jax.ShapeDtypeStruct((TOK, D), BF16),
+        in_specs=[VMEM_SPEC, pl.BlockSpec(memory_space=pl.ANY)],
+        out_specs=VMEM_SPEC,
+        compiler_params=params(2),
+        name="relay",
+    )(far, mark)
+    chip_far = lax.ppermute(far, AXES, chip_pairs)
+    near, value = pl.pallas_call(
+        beside_kernel,
+        out_shape=(score_type, value_type),
+        in_specs=[VMEM_SPEC] * 10,
+        out_specs=(VMEM_SPEC,) * 2,
+        compiler_params=params(14),
+        name="beside_windows",
+    )(shifts, both, far, early, mark, query, early_value, attn_gain, wk, wv_t)
     merged = pl.pallas_call(
         block_kernel,
         out_shape=jax.ShapeDtypeStruct((WH // 2, WW // 2, LATENT, w_merge.shape[1]), BF16),

time: 33.5 us -> 33.4 us (level)
  waiting for transfers between devices: 1.06 us -> 0.38 us
  Pallas kernels: 13.8 us -> 14.3 us
    ppermute x1, waiting for transfers between devices: 1.04 us -> 0.01 us  [on_device(): far = lax.ppermute(other, AXES, far_pairs)]
    pallas_call x1 -> x3, Pallas kernels: 2.45 us -> 2.91 us  [the longest x1 1.95 us: on_device(): pl.pallas_call(early_kernel, out_shape=(score_type, pltpu.VMEM((TOK, PACK...]
    ppermute x1, waiting for transfers between devices: 0.01 us -> 0.37 us  [on_device(): chip_far = lax.ppermute(far, AXES, chip_pairs)]
  transfers between devices with their start and end apart: 6 -> 6, of which waited for: 1 -> 1; matrix products, arithmetic and copies ran while one was open for 0% -> 0% of each run, Pallas kernels for 22% -> 24%
where the time goes in v6:
time: 33.4 us; the launch traced here: 33.3 us
  starting transfers between devices  17.2 us (51%)
  Pallas kernels  14.3 us (43%)
  between operations  1.43 us (4%)
  waiting for transfers between devices  0.38 us (1%)
    ppermute x1, starting transfers between devices, on_device(): cross_far = lax.ppermute(own, AXES, corner_pairs)  8.33 us
    pallas_call x1, Pallas kernels, on_device(): pl.pallas_call(block_kernel, out_shape=jax.ShapeDtypeStruct((WH // 2, WW...  4.98 us
    pallas_call x1, Pallas kernels, on_device(): pl.pallas_call(local_kernel, out_shape=(pltpu.VMEM((positions, LATENT * H...  4.9 us
    ppermute x1, starting transfers between devices, on_device(): cross_both = lax.ppermute(both, AXES, cross_pairs)  2.89 us
    ppermute x1, starting transfers between devices, on_device(): far_levels = lax.ppermute(levels_in, AXES, level_pairs)  2.13 us
    ppermute x1, starting transfers between devices, on_device(): chip_both = lax.ppermute(both, AXES, chip_pairs)  2 us
    pallas_call x1, Pallas kernels, on_device(): pl.pallas_call(early_kernel, out_shape=(score_type, pltpu.VMEM((TOK, PACK...  1.95 us
    ppermute x1, starting transfers between devices, on_device(): far = lax.ppermute(other, AXES, far_pairs)  1.71 us
  transfers between devices with their start and end apart: 6, of which 1 were waited for; matrix products, arithmetic and copies ran while one was open for 0% of the time, Pallas kernels for 24%

profile of v6, /device:TPU:1, one launch (start us, length us, event | category | flops | bytes accessed | tf_op | source)
XLA Modules:
  0.0 33.3 jit_solution(6835735331648699890)
XLA Ops:
  0.0 2.1 %collective-permute-start = (bf16[2,6,24,512]{3,2,1,0:T(8,128)(2,1)}, bf16[2,6,24,512]{3,2,1,0:T(8,128)(2,1)S(1)}, u32[]{:S(2)}, u32[]{:S(2)}) collective-permute-start(bf16[2,6,24,512]{3,2,1,0:T(8,128)(2,1)} %levels_hbm.1), channel_id=1, source_target_pairs={{0,1},{1,0},{2,3},{3,2},{4,5},{5,4},{6,7},{7,6},{8,9},{9,8},{10,11... | collective-permute-start | bytes 884744 | tf_op jit(solution)/shard_map/ppermute | solution.py:454
  3.4 0.0 copy-start.1
  3.4 0.0 copy-start.3
  3.4 4.9 %local_levels.1 = (f32[288,32]{1,0:T(8,128)S(1)}, bf16[288,512]{1,0:T(8,128)(2,1)S(1)}, bf16[32,512]{1,0:T(8,128)(2,1)S(1)}, bf16[512,512]{1,0:T(8,128)(2,1)S(1)...) custom-call(s32[1]{0:T(128)S(6)} %copy.17.shift_lat_ref, ...), custom_call_target="tpu_custom_call" | custom-call | tf_op jit(solution)/shard_map/local_levels/pallas_call | solution.py:459
  8.3 0.0 copy-start
  8.4 0.0 collective-permute-done.levels_ref
  8.4 0.0 copy-done.1
  8.4 0.0 copy-done.3
  8.4 1.5 %encode.1.both_ref = bf16[288,512]{1,0:T(8,128)(2,1)S(1)} custom-call(bf16[2,6,24,512]{3,2,1,0:T(8,128)(2,1)S(1)} %collective-permute-done.levels_ref, f32[288,32]{1,0:T(8,128)S(1)} %get-tuple-element.27.score_ref, bf16[288,512]{1,0:T(8,128)(2,1)S(1)} %get-tuple-element.28.value_ref, bf16[32,512]{1,0:T(8,128)(2,1)S(1)} %get-tuple-element.29.query_ref, ...), custom_call_target="tpu_custom_call" | custom-call | tf_op jit(solution)/shard_map/encode/pallas_call | solution.py:491
  9.9 2.0 %collective-permute-start.1 = (bf16[288,512]{1,0:T(8,128)(2,1)S(1)}, bf16[288,512]{1,0:T(8,128)(2,1)S(1)}, u32[]{:S(2)}, u32[]{:S(2)}) collective-permute-start(bf16[288,512]{1,0:T(8,128)(2,1)S(1)} %encode.1.both_ref), channel_id=1, source_target_pairs={{0,64},{1,65},{2,66},{3,67},{4,68},{5,69},{6,70},{7,71},{8,72},{9,... | collective-permute-start | bytes 884744 | tf_op jit(solution)/shard_map/ppermute | solution.py:499
  11.9 2.9 %collective-permute-start.3 = (bf16[288,512]{1,0:T(8,128)(2,1)S(1)}, bf16[288,512]{1,0:T(8,128)(2,1)S(1)}, u32[]{:S(2)}, u32[]{:S(2)}) collective-permute-start(bf16[288,512]{1,0:T(8,128)(2,1)S(1)} %encode.1.both_ref), channel_id=1, source_target_pairs={{0,1},{1,0},{2,3},{3,2},{4,5},{5,4},{6,7},{7,6},{8,9},{9,8},{10,11... | collective-permute-start | bytes 884744 | tf_op jit(solution)/shard_map/ppermute | solution.py:500
  14.8 0.0 collective-permute-done.1.chip_ref
  14.8 1.7 %collective-permute-start.2 = (bf16[144,512]{1,0:T(8,128)(2,1)S(1)}, bf16[144,512]{1,0:T(8,128)(2,1)S(1)}, u32[]{:S(2)}, u32[]{:S(2)}) collective-permute-start(bf16[144,512]{1,0:T(8,128)(2,1)S(1)} %get-tuple-element.32), channel_id=1, source_target_pairs={{0,2},{1,63},{2,4},{3,1},{4,6},{5,3},{6,8},{7,5},{8,10},{9,7},{10,... | collective-permute-start | bytes 442376 | tf_op jit(solution)/shard_map/ppermute | solution.py:509
  16.5 8.3 %collective-permute-start.5 = (bf16[144,512]{1,0:T(8,128)(2,1)S(1)}, bf16[144,512]{1,0:T(8,128)(2,1)S(1)}, u32[]{:S(2)}, u32[]{:S(2)}) collective-permute-start(bf16[144,512]{1,0:T(8,128)(2,1)S(1)} %get-tuple-element.37), channel_id=1, source_target_pairs={{0,1},{1,0},{2,3},{3,2},{4,5},{5,4},{6,7},{7,6},{8,9},{9,8},{10,11... | collective-permute-start | bytes 442376 | tf_op jit(solution)/shard_map/ppermute | solution.py:510
  24.8 0.0 collective-permute-done.3.cross_ref
  24.8 0.0 copy-done
  24.8 2.0 %early_windows.1 = (f32[2,144,1152]{2,1,0:T(8,128)S(1)}, f32[144,1152]{1,0:T(8,128)S(1)}, bf16[512,1152]{1,0:T(8,128)(2,1)S(1)}, bf16[2048,144]{1,0:T(8,128)(2,1)S(1)}) custom-call(s32[8,128]{1,0:T(8,128)S(1)} %get-tuple-element.26.shift_ref, bf16[288,512]{1,0:T(8,128)(2,1)S(1)} %encode.1.both_ref, bf16[288,512]{1,0:T(8,128)(2,1)S(1)} %collective-permute-done.1.chip_ref, ...), custom_call_target="tpu_custom_call" | custom-call | tf_op jit(solution)/shard_map/early_windows/pallas_call | solution.py:513
  26.8 0.0 collective-permute-done.2.far_ref
  26.8 0.1 collective-permute-start.4
  26.9 0.0 copy-start.2
  26.9 0.0 copy-start.4
  27.0 0.9 %beside_windows.1 = (f32[2,144,1152]{2,1,0:T(8,128)S(1)}, bf16[2048,144]{1,0:T(8,128)(2,1)S(1)}) custom-call(s32[8,128]{1,0:T(8,128)S(1)} %get-tuple-element.26.shift_ref, bf16[288,512]{1,0:T(8,128)(2,1)S(1)} %encode.1.both_ref, bf16[144,512]{1,0:T(8,128)(2,1)S(1)} %relay.1.far_ref, f32[2,144,1152]{2,1,0:T(8,128)S(1)} %get-tuple-element.38.score_in_ref, ...), custom_call_target="tpu_custom_call" | custom-call | tf_op jit(solution)/shard_map/beside_windows/pallas_call | solution.py:535
  27.9 0.0 collective-permute-done.5.cross_far_ref
  27.9 0.4 %collective-permute-done.4.chip_far_ref = bf16[144,512]{1,0:T(8,128)(2,1)S(1)} collective-permute-done((bf16[144,512]{1,0:T(8,128)(2,1)S(1)}, bf16[144,512]{1,0:T(8,128)(2,1)S(1)}, u32[]{:S(2)}, u32[]{:S(2)}) %collective-permute-start.4) | collective-permute-done | bytes 147488 | tf_op jit(solution)/shard_map/ppermute | solution.py:534
  28.3 0.0 copy-done.2
  28.3 0.0 copy-done.4
  28.3 5.0 %window_block.1 = bf16[3,6,2,1024]{3,2,1,0:T(2,128)(2,1)} custom-call(s32[8,128]{1,0:T(8,128)S(1)} %get-tuple-element.26.shift_ref, bf16[288,512]{1,0:T(8,128)(2,1)S(1)} %encode.1.both_ref, bf16[288,512]{1,0:T(8,128)(2,1)S(1)} %collective-permute-done.1.chip_ref, bf16[144,512]{1,0:T(8,128)(2,1)S(1)} %collective-permute-done.4.chip_far_ref, ...), custom_call_target="tpu_custom_call" | custom-call | tf_op jit(solution)/shard_map/window_block/pallas_call | solution.py:543
  (2 shorter events, 0.0 us)
Async XLA Ops:
  0.0 8.4 %collective-permute-start = (bf16[2,6,24,512]{3,2,1,0:T(8,128)(2,1)}, bf16[2,6,24,512]{3,2,1,0:T(8,128)(2,1)S(1)}, u32[]{:S(2)}, u32[]{:S(2)}) collective-permute-start(bf16[2,6,24,512]{3,2,1,0:T(8,128)(2,1)} %levels_hbm.1), channel_id=1, source_target_pairs={{0,1},{1,0},{2,3},{3,2},{4,5},{5,4},{6,7},{7,6},{8,9},{9,8},{10,11... | collective-permute-start | bytes 884744 | tf_op jit(solution)/shard_map/ppermute | solution.py:454
  3.4 4.9 %copy-start.1 = (bf16[2,512]{1,0:T(2,128)(2,1)S(1)}, bf16[2,512]{1,0:T(2,128)(2,1)}, u32[]{:S(2)}) copy-start(bf16[2,512]{1,0:T(2,128)(2,1)} %lq_ref.1) | copy-start | bytes 6148
  3.4 4.9 %copy-start.3 = (bf16[512]{0:T(512)(128)(2,1)S(1)}, bf16[512]{0:T(512)(128)(2,1)}, u32[]{:S(2)}) copy-start(bf16[512]{0:T(512)(128)(2,1)} %gain_ref.3) | copy-start | bytes 3076
  8.3 16.5 %copy-start = (bf16[512]{0:T(512)(128)(2,1)S(1)}, bf16[512]{0:T(512)(128)(2,1)}, u32[]{:S(2)}) copy-start(bf16[512]{0:T(512)(128)(2,1)} %attn_gain_ref.1) | copy-start | bytes 3076
  9.9 4.9 %collective-permute-start.1 = (bf16[288,512]{1,0:T(8,128)(2,1)S(1)}, bf16[288,512]{1,0:T(8,128)(2,1)S(1)}, u32[]{:S(2)}, u32[]{:S(2)}) collective-permute-start(bf16[288,512]{1,0:T(8,128)(2,1)S(1)} %encode.1.both_ref), channel_id=1, source_target_pairs={{0,64},{1,65},{2,66},{3,67},{4,68},{5,69},{6,70},{7,71},{8,72},{9,... | collective-permute-start | bytes 884744 | tf_op jit(solution)/shard_map/ppermute | solution.py:499
  11.9 13.0 %collective-permute-start.3 = (bf16[288,512]{1,0:T(8,128)(2,1)S(1)}, bf16[288,512]{1,0:T(8,128)(2,1)S(1)}, u32[]{:S(2)}, u32[]{:S(2)}) collective-permute-start(bf16[288,512]{1,0:T(8,128)(2,1)S(1)} %encode.1.both_ref), channel_id=1, source_target_pairs={{0,1},{1,0},{2,3},{3,2},{4,5},{5,4},{6,7},{7,6},{8,9},{9,8},{10,11... | collective-permute-start | bytes 884744 | tf_op jit(solution)/shard_map/ppermute | solution.py:500
  14.8 12.0 %collective-permute-start.2 = (bf16[144,512]{1,0:T(8,128)(2,1)S(1)}, bf16[144,512]{1,0:T(8,128)(2,1)S(1)}, u32[]{:S(2)}, u32[]{:S(2)}) collective-permute-start(bf16[144,512]{1,0:T(8,128)(2,1)S(1)} %get-tuple-element.32), channel_id=1, source_target_pairs={{0,2},{1,63},{2,4},{3,1},{4,6},{5,3},{6,8},{7,5},{8,10},{9,7},{10,... | collective-permute-start | bytes 442376 | tf_op jit(solution)/shard_map/ppermute | solution.py:509
  16.5 11.4 %collective-permute-start.5 = (bf16[144,512]{1,0:T(8,128)(2,1)S(1)}, bf16[144,512]{1,0:T(8,128)(2,1)S(1)}, u32[]{:S(2)}, u32[]{:S(2)}) collective-permute-start(bf16[144,512]{1,0:T(8,128)(2,1)S(1)} %get-tuple-element.37), channel_id=1, source_target_pairs={{0,1},{1,0},{2,3},{3,2},{4,5},{5,4},{6,7},{7,6},{8,9},{9,8},{10,11... | collective-permute-start | bytes 442376 | tf_op jit(solution)/shard_map/ppermute | solution.py:510
  26.8 1.5 %collective-permute-start.4 = (bf16[144,512]{1,0:T(8,128)(2,1)S(1)}, bf16[144,512]{1,0:T(8,128)(2,1)S(1)}, u32[]{:S(2)}, u32[]{:S(2)}) collective-permute-start(bf16[144,512]{1,0:T(8,128)(2,1)S(1)} %relay.1.far_ref), channel_id=1, source_target_pairs={{0,64},{1,65},{2,66},{3,67},{4,68},{5,69},{6,70},{7,71},{8,72},{9,... | collective-permute-start | bytes 442376 | tf_op jit(solution)/shard_map/ppermute | solution.py:534
  26.9 1.4 %copy-start.2 = (bf16[2048]{0:T(1024)(128)(2,1)S(1)}, bf16[2048]{0:T(1024)(128)(2,1)}, u32[]{:S(2)}) copy-start(bf16[2048]{0:T(1024)(128)(2,1)} %merge_gain_ref.1) | copy-start | bytes 12292
  26.9 1.4 %copy-start.4 = (bf16[512]{0:T(512)(128)(2,1)S(1)}, bf16[512]{0:T(512)(128)(2,1)}, u32[]{:S(2)}) copy-start(bf16[512]{0:T(512)(128)(2,1)} %mlp_gain_ref.1) | copy-start | bytes 3076
